TPU v7x, 128 devices: a whole 4x4x4 slice. The times are simulated.
128 devices in a mesh: range: 8 (over y, core), chan: 16 (over x, z).
Axes of the slice: x: 4, y: 4, z: 4, core: 2. Of those that a mesh axis runs over, the one named last changes fastest.
Arguments:
- echoes: float32 [2, 64, 512, 2048], P(None, 'chan', None, 'range'), may hold values from -18 to 18
- chirp: float32 [2, 129], replicated, may hold values from -0.375 to 0.375
- train_mask: int32 [512, 16], P('chan', 'range'), may hold values from 0 to 1, as said below
Outputs:
- spectra: bfloat16 [2, 512, 64, 2048], P(None, 'chan', None, 'range')
- factors: float32 [512, 2, 128, 128], P('chan')
Inputs may be any that keep to these rules, and one draw needn't show every extreme that they name: `train_mask`: in each Doppler bin exactly 4 consecutive tiles are 0 and all other tiles are 1.
All inputs are finite; a program needn't handle non-finite values.
Results may differ from a plain program's by a relative error of at most 0.001.
Values sent between devices are 32-bit elements; how exact they have to be, the bound alone decides.
No kernel may reach another device: no remote copies, remote signals or barrier semaphores. Data moves between devices by JAX's collectives and lax.ppermute only.
A program may use at most 128 MiB of HBM per device.

v0:
```python
import math

import jax
import jax.numpy as jnp
from jax import lax
from jax.sharding import PartitionSpec as P

TILE = 128


best_precision = lax.Precision.HIGHEST


def from_behind(value, axis, steps):
    count = lax.axis_size(axis)
    leading, last = (max(0, -steps), min(count, count - steps))
    return lax.ppermute(value, axis, [(source, source + steps) for source in range(leading, last)])


def from_behind_2(block, axis, distance):
    devices = range(lax.axis_size(axis))
    route = [((i - distance) % len(devices), i) for i in devices]
    return lax.ppermute(block, axis, route)


def toeplitz_rows(taps):
    tap_span = taps.shape[-1] - 1
    padded = jnp.concatenate([taps, jnp.zeros((taps.shape[0], tap_span), taps.dtype)], -1)
    tiled = jnp.tile(padded, (1, tap_span))
    return tiled[:, : 2 * tap_span * tap_span].reshape(taps.shape[0], tap_span, 2 * tap_span)


def compress(extended, taps):
    tap_span = taps.shape[-1] - 1
    lead_shape = extended.shape[:-1]
    block_count = extended.shape[-1] // tap_span - 1
    blocks = extended.reshape(lead_shape + (block_count + 1, tap_span))
    window = jnp.concatenate([blocks[..., :block_count, :], blocks[..., 1:, :]], -1)
    kernel = toeplitz_rows(taps)
    products = jnp.einsum(
        "tcpnk,sok->tscpno",
        window,
        kernel,
        precision=best_precision,
        preferred_element_type=jnp.float32,
    )
    real_part = products[0, 0] + products[1, 1]
    imag_part = products[1, 0] - products[0, 1]
    return jnp.stack([real_part, imag_part]).reshape(lead_shape + (block_count * tap_span,))


def doppler_table(bin_numbers, pulse_count):
    phase_index = (
        bin_numbers[:, None] * jnp.arange(pulse_count, dtype=jnp.int32)[None, :] % pulse_count
    )
    angles = phase_index.astype(jnp.float32) * (2.0 * math.pi / pulse_count)
    scaling = 1.0 / math.sqrt(pulse_count)
    return jnp.stack([jnp.cos(angles) * scaling, -jnp.sin(angles) * scaling])


def doppler(signal, dft_table):
    products = jnp.einsum(
        "sdp,tcpg->stdcg",
        dft_table,
        signal,
        precision=best_precision,
        preferred_element_type=jnp.float32,
    )
    return jnp.stack([products[0, 0] - products[1, 1], products[0, 1] + products[1, 0]])


def gram_block(spectra_now, spectra_next, weights, scaling):
    snapshot = jnp.concatenate([spectra_now, spectra_next], 2)
    masked = snapshot * weights[None, :, None, :]
    products = jnp.einsum(
        "tbkg,sblg->btskl",
        masked,
        snapshot,
        precision=best_precision,
        preferred_element_type=jnp.float32,
    )
    real_part = products[:, 0, 0] + products[:, 1, 1]
    imag_part = products[:, 0, 1] - products[:, 1, 0]
    return jnp.stack([real_part, imag_part], 1) * scaling


def factor(gram):
    order_size = gram.shape[-1]
    strip_size = min(16, order_size)
    columns = jnp.arange(order_size, dtype=jnp.int32)
    remaining = gram
    pieces = []
    for offset in range(0, order_size, strip_size):
        strip_rows = remaining[:, :, :strip_size, :]

        def column_step(position, carry):
            strip_now, found_rows = carry
            place = offset + position
            row_now = lax.dynamic_index_in_dim(strip_now, position, 2, keepdims=False)
            pivots = jnp.sum(jnp.where(columns == place, row_now[:, 0], 0.0), -1)
            inverse = lax.rsqrt(pivots)[:, None]
            row_real = jnp.where(columns >= place, row_now[:, 0] * inverse, 0.0)
            row_imag = jnp.where(columns > place, row_now[:, 1] * inverse, 0.0)
            coef_real = row_real[:, offset : offset + strip_size]
            coef_imag = row_imag[:, offset : offset + strip_size]
            new_real = (
                strip_now[:, 0]
                - coef_real[:, :, None] * row_real[:, None, :]
                - coef_imag[:, :, None] * row_imag[:, None, :]
            )
            new_imag = (
                strip_now[:, 1]
                - coef_real[:, :, None] * row_imag[:, None, :]
                + coef_imag[:, :, None] * row_real[:, None, :]
            )
            found_rows = lax.dynamic_update_index_in_dim(
                found_rows, jnp.stack([row_real, row_imag], 1), position, 2
            )
            return (jnp.stack([new_real, new_imag], 1), found_rows)

        strip_end, found_rows = lax.fori_loop(
            0, strip_size, column_step, (strip_rows, jnp.zeros_like(strip_rows))
        )
        pieces.append(found_rows)
        if offset + strip_size < order_size:
            tail_part = found_rows[:, :, :, offset + strip_size :]
            products = jnp.einsum(
                "nabi,ncbj->nacij",
                tail_part,
                found_rows,
                precision=best_precision,
                preferred_element_type=jnp.float32,
            )
            update_real = products[:, 0, 0] + products[:, 1, 1]
            update_imag = products[:, 0, 1] - products[:, 1, 0]
            remaining = remaining[:, :, strip_size:, :] - jnp.stack([update_real, update_imag], 1)
    return jnp.concatenate(pieces, 2)


def on_device(echoes, chirp, train_mask):
    tap_span = chirp.shape[-1] - 1
    pulses = echoes.shape[2]
    gate_count = echoes.shape[3]
    rim_gates = from_behind(echoes[..., :tap_span], "range", -1)
    compressed = compress(jnp.concatenate([echoes, rim_gates], -1), chirp)
    spectra_all = doppler(compressed, doppler_table(jnp.arange(pulses, dtype=jnp.int32), pulses))
    turned = lax.all_to_all(spectra_all, "chan", split_axis=1, concat_axis=2, tiled=True)
    edge_bin = from_behind_2(turned[:, :1], "chan", -1)
    following = jnp.concatenate([turned[:, 1:], edge_bin], 1)
    spectra_out = turned.astype(jnp.bfloat16)
    total_gates = gate_count * lax.axis_size("range")
    scaling = 1.0 / total_gates
    weights = jnp.broadcast_to(
        train_mask.astype(jnp.float32)[:, :, None], train_mask.shape + (TILE,)
    ).reshape(train_mask.shape[0], gate_count)
    summed = lax.psum(gram_block(turned, following, weights, scaling), "range")
    factors = factor(summed)
    return (spectra_out, factors)


def solution(mesh):
    return jax.shard_map(
        on_device,
        mesh=mesh,
        in_specs=(P(None, "chan", None, "range"), P(), P("chan", "range")),
        out_specs=(P(None, "chan", None, "range"), P("chan", None, None, None)),
        check_vma=False,
    )
```

profile of v0, /device:TPU:0, one launch (start us, length us, event | category | flops | bytes accessed | tf_op | source)
XLA Modules:
  0.0 498.2 jit_solution(1872627961129438087)
XLA Ops:
  35.3 5.3 %copy.278 = f32[2,4,512,2,128]{4,2,3,1,0:T(8,128)} copy(f32[2,4,512,2,128]{2,4,3,1,0:T(8,128)} %get-tuple-element.1106) | data formatting | bytes 8388608
  40.7 12.5 %fusion.51 = f32[2,2,4,512,2,128]{3,5,4,2,0,1:T(8,128)S(1)} fusion(f32[2,4,512,2,128]{4,2,3,1,0:T(8,128)} %copy.279, f32[2,4,512,2,128]{4,2,3,1,0:T(8,128)} %copy.278, f32[1,2,128,256]{3,1,2,0:T(2,128)S(1)} %bitcast.424), kind=kOutput, calls=%fused_computation.191 | convolution fusion | flops 6444548096 | bytes 17039360 | tf_op jit(solution)/shard_map/tcpnk,sok->tscpno/dot_general | solution.py:40
  54.4 13.9 %fusion.50 = f32[2,2,512,4,256]{2,4,0,3,1:T(8,128)S(1)} fusion(f32[1,4,512,256]{2,3,1,0:T(8,128)S(1)} %bitcast.385, f32[1,4,512,256]{2,3,1,0:T(8,128)S(1)} %bitcast.384, f32[1,512,512]{2,1,0:T(8,128)S(1)} %get-tuple-element.1120, f32[1,512,512]{2,1,0:T(8,128)S(1)} %get-tuple-element.1121), kind=kOutput, calls=%fused_computation.183 | convolution fusion | flops 12886474752 | bytes 14680064 | tf_op jit(solution)/shard_map/sdp,tcpg->stdcg/dot_general | solution.py:62
  71.7 5.4 %copy.192 = f32[2,512,4,256]{3,2,0,1:T(4,128)} copy(f32[2,512,4,256]{1,3,2,0:T(8,128)} %pad_maximum_fusion.9) | data formatting | bytes 8388608 | tf_op jit(solution)/shard_map/stack | solution.py:69
  77.2 39.8 %all_to_all.18 = f32[2,512,4,256]{3,2,0,1:T(4,128)S(1)} all-to-all(f32[2,512,4,256]{3,2,0,1:T(4,128)} %copy.192), channel_id=1, replica_groups=mesh['range'=8,'chan'=16] {'chan'}, dimensions={1} | all-to-all | bytes 8388608 | tf_op jit(solution)/shard_map/all_to_all | solution.py:147
  123.0 5.4 %all_to_all.16 = f32[2,32,64,256]{3,2,0,1:T(8,128)} reshape(f32[2,32,16,4,256]{4,3,2,0,1:T(4,128)} %copy.194) | data formatting | bytes 8388608 | tf_op jit(solution)/shard_map/all_to_all | solution.py:147
  131.1 5.4 %collective-permute-done.1 = f32[2,1,64,256]{3,2,0,1:T(8,128)S(1)} collective-permute-done((f32[2,1,64,256]{3,2,0,1:T(8,128)S(1)}, f32[2,1,64,256]{3,2,0,1:T(8,128)S(1)}, u32[]{:S(2)}, u32[]{:S(2)}) %collective-permute-start.1) | collective-permute-done | bytes 131104 | tf_op jit(solution)/shard_map/ppermute | solution.py:23
  136.5 13.2 %fusion.52 = f32[32,2,2,128,128]{3,4,1,2,0:T(8,128)S(1)} fusion(f32[2,1,64,256]{3,2,0,1:T(8,128)S(1)} %collective-permute-done.1, f32[2,31,64,256]{3,2,0,1:T(8,128)S(1)} %slice-done, f32[2,32,64,256]{3,2,0,1:T(8,128)} %all_to_all.16, f32[32,256]{1,0:T(8,128)S(1)} %bitcast.428), kind=kOutput, calls=%fused_computation.192 | convolution fusion | flops 6452936704 | bytes 16809984 | tf_op jit(solution)/shard_map/tbkg,sblg->btskl/dot_general | solution.py:75
  156.6 106.9 %all-reduce.3.cloned.1.call-done = f32[32,2,128,128]{2,3,0,1:T(8,128)} async-done(((f32[32,2,128,128]{2,3,0,1:T(8,128)}), f32[32,2,128,128]{2,3,0,1:T(8,128)}) %all-reduce.3.cloned.1.call-update) | async-done | bytes 4194320 | tf_op jit(solution)/shard_map/psum | solution.py:156
  266.4 10.7 %while.136 = (s32[]{:T(128)}, f32[32,2,16,128]{3,2,1,0:T(8,128)S(1)}, f32[32,2,16,128]{3,0,1,2:T(8,128)S(1)}, s32[]{:T(128)}) while((s32[]{:T(128)}, f32[32,2,16,128]{3,2,1,0:T(8,128)S(1)}, f32[32,2,16,128]{3,0,1,2:T(8,128)S(1)}, s32[]{:T(128)}) %tuple.405), condition=%wide.region_3.4_spmd.clone.clone, body=%wide.region_1.3_spmd.clone.clone.sunk | while | flops 690530 | bytes 2455021 | solution.py:121
  278.2 7.1 %convolution_bitcast_fusion.6 = f32[32,2,2,112,128]{3,4,0,2,1:T(8,128)S(1)} fusion(f32[32,2,16,128,1]{3,0,1,2,4:T(8,128)S(1)} %bitcast.402, f32[32,2,16,128]{3,2,1,0:T(8,128)S(1)} %get-tuple-element.1118), kind=kOutput, calls=%fused_computation.190 | convolution fusion | flops 352321536 | bytes 8388608 | tf_op jit(solution)/shard_map/nabi,ncbj->nacij/dot_general | solution.py:127
  293.4 13.1 %while.137 = (s32[]{:T(128)}, f32[32,2,16,128]{3,2,1,0:T(8,128)S(1)}, f32[32,2,16,128]{3,0,1,2:T(8,128)S(1)}, s32[]{:T(128)}, s32[]{:T(128)}) while((s32[]{:T(128)}, f32[32,2,16,128]{3,2,1,0:T(8,128)S(1)}, f32[32,2,16,128]{3,0,1,2:T(8,128)S(1)}, s32[]{:T(128)}, s32[]{:T(128)}) %tuple.408), condition=%wide.region_6.7_spmd.clone.clone, body=%wide.region_4.6_spmd.clone.clone.sunk | while | flops 690531 | bytes 2455105 | solution.py:121
  307.7 7.0 %convolution_bitcast_fusion.5 = f32[32,2,2,96,128]{3,4,0,2,1:T(8,128)S(1)} fusion(f32[32,2,16,128,1]{3,0,1,2,4:T(8,128)S(1)} %bitcast.403, f32[32,2,16,128]{3,2,1,0:T(8,128)S(1)} %get-tuple-element.1116), kind=kOutput, calls=%fused_computation.189 | convolution fusion | flops 301989888 | bytes 7340032 | tf_op jit(solution)/shard_map/nabi,ncbj->nacij/dot_general | solution.py:127
  322.9 13.2 %while.138 = (s32[]{:T(128)}, f32[32,2,16,128]{3,2,1,0:T(8,128)S(1)}, f32[32,2,16,128]{3,0,1,2:T(8,128)S(1)}, s32[]{:T(128)}, s32[]{:T(128)}) while((s32[]{:T(128)}, f32[32,2,16,128]{3,2,1,0:T(8,128)S(1)}, f32[32,2,16,128]{3,0,1,2:T(8,128)S(1)}, s32[]{:T(128)}, s32[]{:T(128)}) %tuple.411), condition=%wide.region_9.10_spmd.clone.clone, body=%wide.region_7.9_spmd.clone.clone.sunk | while | flops 690531 | bytes 2455105 | solution.py:121
  337.1 7.0 %convolution_bitcast_fusion.4 = f32[32,2,2,80,128]{3,4,0,2,1:T(8,128)S(1)} fusion(f32[32,2,16,128,1]{3,0,1,2,4:T(8,128)S(1)} %bitcast.404, f32[32,2,16,128]{3,2,1,0:T(8,128)S(1)} %get-tuple-element.1114), kind=kOutput, calls=%fused_computation.188 | convolution fusion | flops 251658240 | bytes 6291456 | tf_op jit(solution)/shard_map/nabi,ncbj->nacij/dot_general | solution.py:127
  352.4 13.4 %while.139 = (s32[]{:T(128)}, f32[32,2,16,128]{3,2,1,0:T(8,128)S(1)}, f32[32,2,16,128]{3,0,1,2:T(8,128)S(1)}, s32[]{:T(128)}, s32[]{:T(128)}) while((s32[]{:T(128)}, f32[32,2,16,128]{3,2,1,0:T(8,128)S(1)}, f32[32,2,16,128]{3,0,1,2:T(8,128)S(1)}, s32[]{:T(128)}, s32[]{:T(128)}) %tuple.414), condition=%wide.region_12.13_spmd.clone.clone, body=%wide.region_10.12_spmd.clone.clone.sunk | while | flops 690531 | bytes 2455105 | solution.py:121
  366.8 7.1 %convolution_bitcast_fusion.3 = f32[32,2,2,64,128]{3,4,0,2,1:T(8,128)S(1)} fusion(f32[32,2,16,128,1]{3,0,1,2,4:T(8,128)S(1)} %bitcast.405, f32[32,2,16,128]{3,2,1,0:T(8,128)S(1)} %get-tuple-element.1112), kind=kOutput, calls=%fused_computation.187 | convolution fusion | flops 201326592 | bytes 5242880 | tf_op jit(solution)/shard_map/nabi,ncbj->nacij/dot_general | solution.py:127
  382.1 13.1 %while.140 = (s32[]{:T(128)}, f32[32,2,16,128]{3,2,1,0:T(8,128)S(1)}, f32[32,2,16,128]{3,0,1,2:T(8,128)S(1)}, s32[]{:T(128)}, s32[]{:T(128)}) while((s32[]{:T(128)}, f32[32,2,16,128]{3,2,1,0:T(8,128)S(1)}, f32[32,2,16,128]{3,0,1,2:T(8,128)S(1)}, s32[]{:T(128)}, s32[]{:T(128)}) %tuple.417), condition=%wide.region_15.16_spmd.clone.clone, body=%wide.region_13.15_spmd.clone.clone.sunk | while | flops 690531 | bytes 2455105 | solution.py:121
  396.3 7.0 %convolution_bitcast_fusion.2 = f32[32,2,2,48,128]{3,4,0,2,1:T(8,128)S(1)} fusion(f32[32,2,16,128,1]{3,0,1,2,4:T(8,128)S(1)} %bitcast.406, f32[32,2,16,128]{3,2,1,0:T(8,128)S(1)} %get-tuple-element.1110), kind=kOutput, calls=%fused_computation.186 | convolution fusion | flops 150994944 | bytes 4194304 | tf_op jit(solution)/shard_map/nabi,ncbj->nacij/dot_general | solution.py:127
  411.5 13.2 %while.141 = (s32[]{:T(128)}, f32[32,2,16,128]{3,2,1,0:T(8,128)S(1)}, f32[32,2,16,128]{3,0,1,2:T(8,128)S(1)}, s32[]{:T(128)}, s32[]{:T(128)}) while((s32[]{:T(128)}, f32[32,2,16,128]{3,2,1,0:T(8,128)S(1)}, f32[32,2,16,128]{3,0,1,2:T(8,128)S(1)}, s32[]{:T(128)}, s32[]{:T(128)}) %tuple.420), condition=%wide.region_18.19_spmd.clone.clone, body=%wide.region_16.18_spmd.clone.clone.sunk | while | flops 690531 | bytes 2455105 | solution.py:121
  425.8 7.1 %convolution_bitcast_fusion.1 = f32[32,2,2,32,128]{3,4,0,2,1:T(8,128)S(1)} fusion(f32[32,2,16,128,1]{3,0,1,2,4:T(8,128)S(1)} %bitcast.407, f32[32,2,16,128]{3,2,1,0:T(8,128)S(1)} %get-tuple-element.1108), kind=kOutput, calls=%fused_computation.185 | convolution fusion | flops 100663296 | bytes 3145728 | tf_op jit(solution)/shard_map/nabi,ncbj->nacij/dot_general | solution.py:127
  441.0 13.0 %while.142 = (s32[]{:T(128)}, f32[32,2,16,128]{3,2,1,0:T(8,128)S(1)}, f32[32,2,16,128]{3,0,1,2:T(8,128)S(1)}, s32[]{:T(128)}, s32[]{:T(128)}) while((s32[]{:T(128)}, f32[32,2,16,128]{3,2,1,0:T(8,128)S(1)}, f32[32,2,16,128]{3,0,1,2:T(8,128)S(1)}, s32[]{:T(128)}, s32[]{:T(128)}) %tuple.423), condition=%wide.region_21.22_spmd.clone.clone, body=%wide.region_19.21_spmd.clone.clone.sunk | while | flops 690531 | bytes 2455105 | solution.py:121
  458.0 7.9 %convolution_bitcast_fusion = f32[32,2,2,16,128]{3,4,0,2,1:T(8,128)S(1)} fusion(f32[32,2,16,128,1]{3,0,1,2,4:T(8,128)S(1)} %bitcast.383, f32[32,2,16,128]{2,3,1,0:T(8,128)} %copy.223), kind=kOutput, calls=%fused_computation.184 | convolution fusion | flops 50331648 | bytes 2097152 | tf_op jit(solution)/shard_map/nabi,ncbj->nacij/dot_general | solution.py:127
  474.0 16.0 %while.143 = (s32[]{:T(128)}, f32[32,2,16,128]{3,2,1,0:T(8,128)S(1)}, f32[32,2,16,128]{3,2,1,0:T(8,128)S(1)}, s32[]{:T(128)}, s32[]{:T(128)}, /*index=5*/s32[]{:T(128)}) while((s32[]{:T(128)}, f32[32,2,16,128]{3,2,1,0:T(8,128)S(1)}, f32[32,2,16,128]{3,2,1,0:T(8,128)S(1)}, s32[]{:T(128)}, s32[]{:T(128)}, ...), condition=%wide.region_24.25_spmd.clone.clone, body=%wide.region_22.24_spmd.clone.clone.sunk | while | flops 690531 | bytes 2586185 | solution.py:121
  (1757 shorter events, 213.1 us)
Async XLA Ops:
  7.2 256.4 %all-reduce.3.cloned.1.call-start = ((), (), s32[]{:S(2)}) async-start(), calls=%async_computation.1 | async-start | bytes 8388608 | tf_op jit(solution)/shard_map/psum | solution.py:156
  12.4 4.4 copy-start.8
  15.5 6.4 %collective-permute-start = (f32[2,4,512,128]{2,3,1,0:T(8,128)}, f32[2,4,512,128]{2,3,1,0:T(8,128)}, u32[]{:S(2)}, u32[]{:S(2)}) collective-permute-start(f32[2,4,512,128]{2,3,1,0:T(8,128)} %slice.757), channel_id=1, source_target_pairs={{16,0},{32,16},{48,32},{64,48},{80,64},{96,80},{112,96},{17,1},{33... | collective-permute-start | bytes 6291464 | tf_op jit(solution)/shard_map/ppermute | solution.py:17
  17.4 8.1 %copy-start.7 = (f32[2,32896]{1,0:T(2,128)}, f32[2,32896]{1,0:T(2,128)S(1)}, u32[]{:S(2)}) copy-start(f32[2,32896]{1,0:T(2,128)S(1)} %tile.10) | copy-start | bytes 789508
  35.3 5.3 %slice-start.1 = ((f32[2,32896]{1,0:T(2,128)}), f32[2,32768]{1,0:T(2,128)S(1)}, s32[]{:S(2)}) async-start(f32[2,32896]{1,0:T(2,128)} %copy-done.7), calls=%async_computation.3 | async-start | bytes 524288 | tf_op jit(solution)/shard_map/slice | solution.py:30
  123.0 7.9 %copy-start.9 = (s32[32,2]{0,1:T(2,128)S(1)}, s32[32,2]{0,1:T(2,128)}, u32[]{:S(2)}) copy-start(s32[32,2]{0,1:T(2,128)} %param.21) | copy-start | bytes 772
  129.3 7.2 %collective-permute-start.1 = (f32[2,1,64,256]{3,2,0,1:T(8,128)S(1)}, f32[2,1,64,256]{3,2,0,1:T(8,128)S(1)}, u32[]{:S(2)}, u32[]{:S(2)}) collective-permute-start(f32[2,1,64,256]{3,2,0,1:T(8,128)S(1)} %slice.769), channel_id=1, source_target_pairs={{1,0},{2,1},{3,2},{4,3},{5,4},{6,5},{7,6},{8,7},{9,8},{10,9},{11,1... | collective-permute-start | bytes 393224 | tf_op jit(solution)/shard_map/ppermute | solution.py:23
  131.0 5.5 %slice-start = ((f32[2,32,64,256]{3,2,0,1:T(8,128)}), f32[2,31,64,256]{3,2,0,1:T(8,128)S(1)}, s32[]{:S(2)}) async-start(f32[2,32,64,256]{3,2,0,1:T(8,128)} %all_to_all.16), calls=%async_computation.2 | async-start | bytes 8126464 | tf_op jit(solution)/shard_map/slice | solution.py:149
  285.2 2.2 copy-start.6
  314.7 2.2 copy-start
  344.2 2.2 copy-start.1
  373.9 2.2 copy-start.2
  403.4 2.2 copy-start.3
  432.9 2.2 copy-start.4
  465.9 2.2 copy-start.5
Sparse Core Ops, SparseCore 0:
  152.8 110.7 all-reduce.2
where the time goes:
time: 508 us; the launch traced here: 498 us
  other arithmetic  115 us (23%)
  waiting for transfers between devices  113 us (22%)
  local copies, waits for them, and re-layouts  111 us (22%)
  matrix products  89.8 us (18%)
  blocking collectives  39.8 us (8%)
  between operations  15 us (3%)
  loops' own time  12 us (2%)
    psum x1, waiting for transfers between devices, on_device(): summed = lax.psum(gram_block(turned, following, weights, scaling), 'range')  107 us
    dot_general x7, matrix products, factor(): jnp.einsum('nabi,ncbj->nacij', tail_part, found_rows, precision=best_prec...  50.2 us
    unnamed x34, local copies, waits for them, and re-layouts  48.3 us
    all_to_all x1, blocking collectives, on_device(): lax.all_to_all(spectra_all, 'chan', split_axis=1, concat_axis=2, tiled=True)  39.8 us
    sub x128, other arithmetic, column_step(): strip_now[:, 0] - coef_real[:, :, None] * row_real[:, None, :]  26.4 us
    sub x7, other arithmetic, factor(): remaining[:, :, strip_size:, :] - jnp.stack([update_real, update_imag], 1)  21.8 us
    select_n x256, other arithmetic, column_step(): row_real = jnp.where(columns >= place, row_now[:, 0] * inverse, 0.0)  19.6 us
    reduce_sum x128, other arithmetic, column_step(): pivots = jnp.sum(jnp.where(columns == place, row_now[:, 0], 0.0), -1)  14.2 us
  transfers between devices with their start and end apart: 3, of which 3 were waited for; matrix products, arithmetic and copies ran while one was open for 2% of the time, Pallas kernels for 0%

commit v1 on v0

v1 whole, which is shorter than its diff:
```python
import functools
import math

import jax
import jax.numpy as jnp
import numpy as np
from jax import lax
from jax.experimental import pallas as pl
from jax.experimental.pallas import tpu as pltpu
from jax.sharding import PartitionSpec as P

PULSES = 512
TILE = 128
BINS = 32
WIDE = BINS + 1
CHANS = 16
LOCAL = 4
LATE = 8
EARLY = BINS - LATE
STRIP = 16
F32 = jnp.float32
BF16 = jnp.bfloat16
VMEM = pl.BlockSpec(memory_space=pltpu.VMEM)
SMEM = pl.BlockSpec(memory_space=pltpu.SMEM)
ANY = pl.BlockSpec(memory_space=pl.ANY)


def params(mib=48):
    return pltpu.CompilerParams(vmem_limit_bytes=mib << 20)


def cost(flops, nbytes):
    return pl.CostEstimate(flops=int(flops), bytes_accessed=int(nbytes), transcendentals=0)


def split(value):
    high = value.astype(BF16)
    return high, (value - high.astype(F32)).astype(BF16)


def dot3(left, right, contract=((1,), (0,))):
    lh, ll = left
    rh, rl = right
    dims = (contract, ((), ()))
    dot = functools.partial(lax.dot_general, dimension_numbers=dims, preferred_element_type=F32)
    return dot(lh, rh) + (dot(lh, rl) + dot(ll, rh))


def doppler_matrices():
    rows = np.arange(128)[:, None]
    pulses = np.arange(128)[None, :]
    found = []
    for j in range(4):
        angle = ((4 * rows + j) * pulses % PULSES) * (2.0 * math.pi / PULSES)
        c, s = np.cos(angle), np.sin(angle)
        found.append(np.block([[c, s], [-s, c]]) / math.sqrt(PULSES))
    full = np.stack(found).astype(np.float32)
    high = full.astype(jnp.bfloat16)
    low = (full - high.astype(np.float32)).astype(jnp.bfloat16)
    return np.stack([high, low])


def fill_toeplitz(chirp_ref, pad_ref, kmat_ref):
    pad_ref[...] = jnp.zeros_like(pad_ref)
    pad_ref[0:2, 0 : TILE + 1] = chirp_ref[...]
    taps = []
    for part in range(2):
        row = jnp.broadcast_to(pad_ref[part : part + 1, :], (TILE, 2 * TILE))
        taps.append(pltpu.roll(row, 0, 1, stride=1, stride_axis=0).T)
    re, im = taps
    full = jnp.concatenate(
        [jnp.concatenate([re, -im], 1), jnp.concatenate([im, re], 1)], 0
    )
    kmat_ref[0], kmat_ref[1] = split(full)


def front_body(step, windows, kmat_ref, w_ref, store):
    tables = (kmat_ref[0], kmat_ref[1])
    quarters = [[], [], [], []]
    for window in windows:
        y = dot3(split(window), tables)
        y0, y1, y2, y3 = (y[128 * q : 128 * q + 128] for q in range(4))
        s02, d02, s13, d13 = y0 + y2, y0 - y2, y1 + y3, y1 - y3
        d02r, d02i, d13r, d13i = d02[:, :128], d02[:, 128:], d13[:, :128], d13[:, 128:]
        z0, z2 = s02 + s13, s02 - s13
        quarters[0].append((z0[:, :128], z0[:, 128:]))
        quarters[1].append((d02r + d13i, d02i - d13r))
        quarters[2].append((z2[:, :128], z2[:, 128:]))
        quarters[3].append((d02r - d13i, d02i + d13r))
    for j in range(4):
        (r0, i0), (r1, i1) = quarters[j]
        data = jnp.concatenate(
            [jnp.concatenate([r0, r1], 1), jnp.concatenate([i0, i1], 1)], 0
        )
        out = dot3((w_ref[0, j], w_ref[1, j]), split(data))
        for part in range(2):
            for c in range(2):
                store(j, part, c, out[128 * part : 128 * part + 128, 128 * c : 128 * c + 128])


def store_into(flat_ref, step):
    def store(j, part, c, block):
        for k in range(CHANS):
            start = k * WIDE * 8 + j * 8 + part * 4 + c + 2 * step
            flat_ref[pl.ds(start, 8, stride=32), :] = block[8 * k : 8 * k + 8]

    return store


def add_edges(flat_ref):
    for k in range(CHANS):
        source = ((k + 1) % CHANS) * WIDE * 8
        flat_ref[pl.ds(k * WIDE * 8 + BINS * 8, 8), :] = flat_ref[pl.ds(source, 8), :]


def front0_kernel(chirp_ref, x_ref, w_ref, out_ref, rim_ref, pad_ref, kmat_ref):
    step = pl.program_id(0)

    @pl.when(step == 0)
    def _():
        fill_toeplitz(chirp_ref, pad_ref, kmat_ref)

    windows = []
    for c in range(2):
        windows.append(jnp.concatenate([x_ref[0, c], x_ref[1, c]], 1))
    rim_ref[...] = x_ref[:, :, :, :TILE]
    front_body(step, windows, kmat_ref, w_ref, store_into(out_ref, step))

    @pl.when(step == 1)
    def _():
        add_edges(out_ref)


def front1_kernel(chirp_ref, x_ref, h_ref, w_ref, a_ref, b_ref, pad_ref, kmat_ref, flat_ref):
    step = pl.program_id(0)

    @pl.when(step == 0)
    def _():
        fill_toeplitz(chirp_ref, pad_ref, kmat_ref)

    windows = []
    for c in range(2):
        windows.append(jnp.concatenate([x_ref[0, c], h_ref[0, c], x_ref[1, c], h_ref[1, c]], 1))
    front_body(step, windows, kmat_ref, w_ref, store_into(flat_ref, step))

    @pl.when(step == 1)
    def _():
        add_edges(flat_ref)
        for k in range(CHANS):
            base = k * WIDE * 8
            middle = (EARLY + 1) * 8
            a_ref[k] = flat_ref[pl.ds(base, middle), :]
            b_ref[k] = flat_ref[pl.ds(base + middle, LATE * 8), :]


def front_scratch():
    return [pltpu.VMEM((8, 2 * TILE), F32), pltpu.VMEM((2, 4 * TILE, 2 * TILE), BF16)]


def front0(chirp, echoes, w):
    return pl.pallas_call(
        front0_kernel,
        grid=(2,),
        in_specs=[
            pl.BlockSpec(chirp.shape, lambda i: (0, 0)),
            pl.BlockSpec((2, 2, PULSES, 2 * TILE), lambda i: (0, i, 0, 0)),
            pl.BlockSpec(w.shape, lambda i: (0, 0, 0, 0)),
        ],
        out_specs=[
            pl.BlockSpec((CHANS * WIDE * 8, TILE), lambda i: (0, 0)),
            pl.BlockSpec((2, 2, PULSES, TILE), lambda i: (0, i, 0, 0)),
        ],
        out_shape=[
            jax.ShapeDtypeStruct((CHANS * WIDE * 8, TILE), F32),
            jax.ShapeDtypeStruct((2, LOCAL, PULSES, TILE), F32),
        ],
        scratch_shapes=front_scratch(),
        compiler_params=params(),
        cost_estimate=cost(4e9, 12e6),
        name="front0",
    )(chirp, echoes, w)


def front1(chirp, echoes, rim, w):
    return pl.pallas_call(
        front1_kernel,
        grid=(2,),
        in_specs=[
            pl.BlockSpec(chirp.shape, lambda i: (0, 0)),
            pl.BlockSpec((2, 2, PULSES, TILE), lambda i: (0, i, 0, 1)),
            pl.BlockSpec((2, 2, PULSES, TILE), lambda i: (0, i, 0, 0)),
            pl.BlockSpec(w.shape, lambda i: (0, 0, 0, 0)),
        ],
        out_specs=[
            pl.BlockSpec((CHANS, (EARLY + 1) * 8, TILE), lambda i: (0, 0, 0)),
            pl.BlockSpec((CHANS, LATE * 8, TILE), lambda i: (0, 0, 0)),
        ],
        out_shape=[
            jax.ShapeDtypeStruct((CHANS, (EARLY + 1) * 8, TILE), F32),
            jax.ShapeDtypeStruct((CHANS, LATE * 8, TILE), F32),
        ],
        scratch_shapes=front_scratch() + [pltpu.VMEM((CHANS * WIDE * 8, TILE), F32)],
        compiler_params=params(),
        cost_estimate=cost(4e9, 8e6),
        name="front1",
    )(chirp, echoes, rim, w)


def unweave(blocks):
    pairs = blocks.reshape(CHANS // 2, 2, 8, TILE)
    even, odd = pairs[:, 0], pairs[:, 1]
    first = lax.broadcasted_iota(jnp.int32, even.shape, 1) < 4
    even_turned = pltpu.roll(even, 4, 1)
    odd_turned = pltpu.roll(odd, 4, 1)
    re = jnp.where(first, even, odd_turned).reshape(CHANS * LOCAL, TILE)
    im = jnp.where(first, even_turned, odd).reshape(CHANS * LOCAL, TILE)
    return re, im


def plant(place, blocks, store_spectra, high_ref, low_ref):
    re, im = unweave(blocks)
    rh, rl = split(re)
    ih, il = split(im)
    store_spectra(rh, ih)
    high_ref[0, place] = jnp.concatenate([rh, ih], 1)
    high_ref[1, place] = jnp.concatenate([ih, -rh], 1)
    low_ref[0, place] = jnp.concatenate([rl, il], 1)
    low_ref[1, place] = jnp.concatenate([il, -rl], 1)


def bin_gram(place, high_ref, low_ref):
    def rows(ref, kind):
        return ref[kind, pl.ds(place, 2)].reshape(128, 2 * TILE)

    ah, al = rows(high_ref, 0), rows(low_ref, 0)
    bh = jnp.concatenate([ah, rows(high_ref, 1)], 0)
    bl = jnp.concatenate([al, rows(low_ref, 1)], 0)
    both = dot3((ah, al), (bh, bl), ((1,), (1,)))
    row = lax.broadcasted_iota(jnp.int32, (128, 128), 0)
    column = lax.broadcasted_iota(jnp.int32, (128, 128), 1)
    return jnp.where(row <= column, both[:, :128], both[:, 128:])


def gram0_kernel(mask_ref, r_ref, sums_ref, spectra_ref, high_ref, low_ref):
    def plant_one(b, carry):
        def store(rh, ih):
            @pl.when(b < BINS)
            def _():
                spectra_ref[0, b] = rh
                spectra_ref[1, b] = ih

        plant(b, r_ref[:, b], store, high_ref, low_ref)
        return carry

    lax.fori_loop(0, WIDE, plant_one, 0, unroll=3)

    def one(b, carry):
        weight = mask_ref[b, 0].astype(F32)
        sums_ref[b] = bin_gram(b, high_ref, low_ref) * weight
        return carry

    lax.fori_loop(0, BINS, one, 0, unroll=4)


def gram_scratch(count):
    return [pltpu.VMEM((2, count + 1, 64, 2 * TILE), BF16)] * 2


def gram0(mask, received):
    return pl.pallas_call(
        gram0_kernel,
        in_specs=[SMEM, VMEM],
        out_specs=[
            VMEM,
            pl.BlockSpec((2, BINS, 64, TILE), lambda i: (0, 0, 0, 0)),
        ],
        grid=(1,),
        out_shape=[
            jax.ShapeDtypeStruct((BINS, 128, 128), F32),
            jax.ShapeDtypeStruct((2, BINS, 64, 2 * TILE), BF16),
        ],
        scratch_shapes=gram_scratch(BINS),
        compiler_params=params(),
        cost_estimate=cost(2e9, 6e6),
        name="gram0",
    )(mask, received)


def gram1_kernel(first, count, split_at, spot_ref, mask_ref, sums_ref, *refs):
    pieces = refs[: len(split_at)]
    _, keep_ref, send_ref, spectra_ref, high_ref, low_ref = refs[len(split_at) :]
    place = 0
    for piece, (start, amount) in zip(pieces, split_at):

        def plant_one(i, carry, piece=piece, start=start, place=place):
            def store(rh, ih):
                @pl.when(place + i < count)
                def _():
                    spectra_ref[0, place + i] = rh
                    spectra_ref[1, place + i] = ih

            plant(place + i, piece[:, start + i], store, high_ref, low_ref)
            return carry

        lax.fori_loop(0, amount, plant_one, 0, unroll=min(amount, 4))
        place += amount
    half = count // 2
    core = spot_ref[1]
    for out_ref, base in ((send_ref, (1 - core) * half), (keep_ref, core * half)):

        def one(i, carry, out_ref=out_ref, base=base):
            b = base + i
            weight = mask_ref[first + b, 1].astype(F32)
            out_ref[i] = sums_ref[b] + bin_gram(b, high_ref, low_ref) * weight
            return carry

        lax.fori_loop(0, half, one, 0, unroll=4)


def gram1(first, count, spot, mask, sums, pieces, split_at, spectra, name):
    half = count // 2
    block = first // count
    return pl.pallas_call(
        functools.partial(gram1_kernel, first, count, split_at),
        grid=(1,),
        in_specs=[
            SMEM,
            SMEM,
            pl.BlockSpec((count, 128, 128), lambda i: (block, 0, 0)),
        ]
        + [VMEM] * len(pieces)
        + [ANY],
        out_specs=[VMEM, VMEM, pl.BlockSpec((2, count, 64, TILE), lambda i: (0, block, 0, 1))],
        out_shape=[
            jax.ShapeDtypeStruct((half, 128, 128), F32),
            jax.ShapeDtypeStruct((half, 128, 128), F32),
            jax.ShapeDtypeStruct(spectra.shape, spectra.dtype),
        ],
        scratch_shapes=gram_scratch(count),
        input_output_aliases={3 + len(pieces): 2},
        compiler_params=params(),
        cost_estimate=cost(2e9 * count / 32, 6e6 * count / 32),
        name=name,
    )(spot, mask, sums, *pieces, spectra)


def core_sum_kernel(share, spot_ref, keep_ref, got_ref, *outs):
    for k, out_ref in enumerate(outs):
        base = lax.rem(spot_ref[0] + k, 4) * share
        out_ref[...] = keep_ref[pl.ds(base, share)] + got_ref[pl.ds(base, share)]


def core_sum(spot, keep, got):
    share = keep.shape[0] // 4
    return pl.pallas_call(
        functools.partial(core_sum_kernel, share),
        in_specs=[SMEM, VMEM, VMEM],
        out_specs=[VMEM] * 4,
        out_shape=[jax.ShapeDtypeStruct((share, 128, 128), F32)] * 4,
        compiler_params=params(),
        cost_estimate=cost(1e6, 2e6),
        name="core_sum",
    )(spot, keep, got)


def factor_kernel(scaling, *refs):
    out_ref = refs[-7]
    ins = refs[:-7]
    gre_ref, gim_ref, fre_ref, fim_ref, sre_ref, sim_ref = refs[-6:]
    count = out_ref.shape[0]
    row = lax.broadcasted_iota(jnp.int32, (128, 128), 0)
    column = lax.broadcasted_iota(jnp.int32, (128, 128), 1)
    for n in range(count):
        packed = ins[0][n]
        for more in ins[1:]:
            packed = packed + more[n]
        packed = packed * scaling
        turned = packed.T
        gre_ref[n] = jnp.where(row <= column, packed, turned)
        gim_ref[n] = jnp.where(row < column, -turned, jnp.where(row > column, packed, 0.0))
    high = lax.Precision.HIGHEST
    dims = (((0,), (0,)), ((), ()))
    dot = functools.partial(
        lax.dot_general, dimension_numbers=dims, preferred_element_type=F32, precision=high
    )
    for offset in range(0, 128, STRIP):
        strips = []
        for n in range(count):
            re = gre_ref[n, offset : offset + STRIP]
            im = gim_ref[n, offset : offset + STRIP]
            if offset:
                fr, fi = fre_ref[n, :offset], fim_ref[n, :offset]
                lr, li = fr[:, offset : offset + STRIP], fi[:, offset : offset + STRIP]
                both = jnp.concatenate([fr, fi], 0)
                re = re - dot(jnp.concatenate([lr, li], 0), both)
                im = im - dot(jnp.concatenate([-li, lr], 0), both)
            strips.append((re, im))
        for i in range(STRIP):
            place = offset + i
            later = []
            for n, (re, im) in enumerate(strips):
                col_re = re[:, place : place + 1]
                col_im = im[:, place : place + 1]
                pivot = re[i : i + 1, place : place + 1]
                inverse = lax.rsqrt(pivot)
                row_re = re[i : i + 1] * inverse
                row_im = im[i : i + 1] * inverse
                fre_ref[n, place : place + 1] = row_re
                fim_ref[n, place : place + 1] = row_im
                if i + 1 < STRIP:
                    cr = col_re * inverse
                    ci = col_im * inverse
                    re, im = (
                        re - (cr * row_re - ci * row_im),
                        im - (cr * row_im + ci * row_re),
                    )
                later.append((re, im))
            strips = later
        for n in range(count):
            fre = fre_ref[n, offset : offset + STRIP]
            fim = fim_ref[n, offset : offset + STRIP]
            r = lax.broadcasted_iota(jnp.int32, (STRIP, 128), 0) + offset
            c = lax.broadcasted_iota(jnp.int32, (STRIP, 128), 1)
            fre_ref[n, offset : offset + STRIP] = jnp.where(c >= r, fre, 0.0)
            fim_ref[n, offset : offset + STRIP] = jnp.where(c > r, fim, 0.0)
    for n in range(count):
        out_ref[n] = fre_ref[n] + fim_ref[n].T


def factor(pieces, scaling):
    count = pieces[0].shape[0]
    return pl.pallas_call(
        functools.partial(factor_kernel, scaling),
        in_specs=[VMEM] * len(pieces),
        out_specs=VMEM,
        out_shape=jax.ShapeDtypeStruct((count, 128, 128), F32),
        scratch_shapes=[pltpu.VMEM((count, 128, 128), F32)] * 4
        + [pltpu.VMEM((count, STRIP, 128), F32)] * 2,
        compiler_params=params(),
        cost_estimate=cost(8e9, 2e6),
        name="factor",
    )(*pieces)


def unpack_kernel(share, spot_ref, *refs):
    pieces, out_ref = refs[:8], refs[-1]
    row = lax.broadcasted_iota(jnp.int32, (128, 128), 0)
    column = lax.broadcasted_iota(jnp.int32, (128, 128), 1)
    y, core = spot_ref[0], spot_ref[1]
    for k in range(8):
        steps, other = k % 4, k // 4
        owner = lax.rem(y + 4 - steps, 4)
        whose = core + other - 2 * core * other
        base = (whose * 4 + owner) * share

        def one(i, carry, piece=pieces[k], base=base):
            packed = piece[i]
            out_ref[base + i, 0] = jnp.where(row <= column, packed, 0.0)
            out_ref[base + i, 1] = jnp.where(row < column, packed.T, 0.0)
            return carry

        lax.fori_loop(0, share, one, 0, unroll=True)


def unpack(first, spot, pieces, below):
    share = pieces[0].shape[0]
    count = share * 8
    block = first // count
    more = [] if below is None else [below]
    return pl.pallas_call(
        functools.partial(unpack_kernel, share),
        grid=(1,),
        in_specs=[SMEM] + [VMEM] * 8 + [ANY] * len(more),
        out_specs=pl.BlockSpec((count, 2, 128, 128), lambda i: (block, 0, 0, 0)),
        out_shape=jax.ShapeDtypeStruct((BINS, 2, 128, 128), F32),
        input_output_aliases={9: 0} if more else {},
        compiler_params=params(),
        cost_estimate=cost(1e6, count * 200e3),
        name="unpack",
    )(spot, *pieces, *more)


def along_y(value, steps):
    return lax.ppermute(value, "range", [(i, (i + 2 * steps) % 8) for i in range(8)])


def other_core(value):
    return lax.ppermute(value, "range", [(i, i ^ 1) for i in range(8)])


def across(value):
    return lax.all_to_all(value, "chan", split_axis=0, concat_axis=0, tiled=True)


def back(spot, keep, send, scaling):
    got = other_core(send)
    own, *rest = core_sum(spot, keep, got)
    parts = [own] + [along_y(piece, k + 1) for k, piece in enumerate(rest)]
    mine = factor(parts, scaling)
    found = [mine] + [along_y(mine, k) for k in (1, 2, 3)]
    return found + [other_core(piece) for piece in found]


def on_device(echoes, chirp, train_mask):
    w = jnp.asarray(doppler_matrices())
    spot_range = lax.axis_index("range").astype(jnp.int32)
    spot = jnp.stack([spot_range // 2, spot_range % 2])
    scaling = 1.0 / (2 * TILE * 8)
    flat0, rim = front0(chirp, echoes, w)
    halo = lax.ppermute(rim, "range", [(i, i - 1) for i in range(1, 8)])
    got0 = across(flat0.reshape(CHANS, WIDE, 8, TILE))
    send_a, send_b = front1(chirp, echoes, halo, w)
    got_a = across(send_a).reshape(CHANS, EARLY + 1, 8, TILE)
    got_b = across(send_b).reshape(CHANS, LATE, 8, TILE)
    sums0, spectra = gram0(train_mask, got0)
    keep_a, out_a, spectra = gram1(
        0, EARLY, spot, train_mask, sums0, [got_a], [(0, EARLY + 1)], spectra, "gram_a"
    )
    pieces_a = back(spot, keep_a, out_a, scaling)
    keep_b, out_b, spectra = gram1(
        EARLY, LATE, spot, train_mask, sums0, [got_a, got_b], [(EARLY, 1), (0, LATE)], spectra, "gram_b"
    )
    pieces_b = back(spot, keep_b, out_b, scaling)
    factors = unpack(0, spot, pieces_a, None)
    factors = unpack(EARLY, spot, pieces_b, factors)
    return spectra, factors


def solution(mesh):
    return jax.shard_map(
        on_device,
        mesh=mesh,
        in_specs=(P(None, "chan", None, "range"), P(), P("chan", "range")),
        out_specs=(P(None, "chan", None, "range"), P("chan", None, None, None)),
        check_vma=False,
    )
```

time: 508 us -> 182 us (0.36); the launches traced: 498 us -> 181 us
  other arithmetic: 115 us -> 0.07 us
  local copies, waits for them, and re-layouts: 111 us -> 11.6 us
  matrix products: 89.8 us -> 0 us
  Pallas kernels: 0 us -> 64.2 us
  waiting for transfers between devices: 113 us -> 51.6 us
  starting transfers between devices: 2.89 us -> 36.9 us
  blocking collectives: 39.8 us -> 15.7 us
  between operations: 15 us -> 0.82 us
  loops' own time: 12 us -> 0 us
    psum x1 -> x0, waiting for transfers between devices: 107 us -> none  [on_device(): summed = lax.psum(gram_block(turned, following, weights, scaling), 'range')]
    dot_general x10 -> x0, matrix products: 89.8 us -> none  [the longest x7 50.2 us: factor(): jnp.einsum('nabi,ncbj->nacij', tail_part, found_rows, precision=best_prec...]
    pallas_call x0 -> x11, Pallas kernels: none -> 64.2 us  [the longest x2 28.6 us: factor(): pl.pallas_call(functools.partial(factor_kernel, scaling), in_specs=[VMEM]...]
    sub x137 -> x0, other arithmetic: 49 us -> none  [the longest x128 26.4 us: column_step(): strip_now[:, 0] - coef_real[:, :, None] * row_real[:, None, :]]
    all_to_all x0 -> x2, waiting for transfers between devices: none -> 37.8 us  [across(): lax.all_to_all(value, 'chan', split_axis=0, concat_axis=0, tiled=True)]
    unnamed x34 -> x23, local copies, waits for them, and re-layouts: 48.3 us -> 11.6 us
    slice x231 -> x0, local copies, waits for them, and re-layouts: 25.3 us -> none  [the longest x112 8.37 us: column_step(): coef_real = row_real[:, offset:offset + strip_size]]
    all_to_all x1, blocking collectives: 39.8 us -> 15.7 us  [across(): lax.all_to_all(value, 'chan', split_axis=0, concat_axis=0, tiled=True)]
  transfers between devices with their start and end apart: 3 -> 25, of which waited for: 3 -> 7; matrix products, arithmetic and copies ran while one was open for 2% -> 0% of each run, Pallas kernels for 0% -> 27%
where the time goes in v1:
time: 182 us; the launch traced here: 181 us
  Pallas kernels  64.2 us (35%)
  waiting for transfers between devices  51.6 us (28%)
  starting transfers between devices  36.9 us (20%)
  blocking collectives  15.7 us (9%)
  local copies, waits for them, and re-layouts  11.6 us (6%)
    all_to_all x2, waiting for transfers between devices, across(): lax.all_to_all(value, 'chan', split_axis=0, concat_axis=0, tiled=True)  37.8 us
    pallas_call x2, Pallas kernels, factor(): pl.pallas_call(functools.partial(factor_kernel, scaling), in_specs=[VMEM]...  28.6 us
    ppermute x12, starting transfers between devices, along_y(): lax.ppermute(value, 'range', [(i, (i + 2 * steps) % 8) for i in range(8)])  19 us
    all_to_all x1, blocking collectives, across(): lax.all_to_all(value, 'chan', split_axis=0, concat_axis=0, tiled=True)  15.7 us
    all_to_all x2, starting transfers between devices, across(): lax.all_to_all(value, 'chan', split_axis=0, concat_axis=0, tiled=True)  15 us
    ppermute x12, waiting for transfers between devices, along_y(): lax.ppermute(value, 'range', [(i, (i + 2 * steps) % 8) for i in range(8)])  13.8 us
    unnamed x23, local copies, waits for them, and re-layouts  11.6 us
    pallas_call x2, Pallas kernels, gram1(): pl.pallas_call(functools.partial(gram1_kernel, first, count, split_at), g...  8.87 us
  transfers between devices with their start and end apart: 25, of which 7 were waited for; matrix products, arithmetic and copies ran while one was open for 0% of the time, Pallas kernels for 27%

profile of v1, /device:TPU:0, one launch (start us, length us, event | category | flops | bytes accessed | tf_op | source)
XLA Modules:
  0.0 180.9 jit_solution(16453669909604947487)
XLA Ops:
  2.5 7.5 %front0.1 = (f32[4224,128]{1,0:T(8,128)S(1)}, f32[2,4,512,128]{3,2,1,0:T(8,128)}) custom-call(f32[2,129]{1,0:T(2,128)S(1)} %copy-done.6, f32[2,4,512,256]{3,2,1,0:T(8,128)} %x_ref.3, bf16[2,4,256,256]{3,2,1,0:T(8,128)(2,1)S(1)} %copy-done.8), custom_call_target="tpu_custom_call" | custom-call | flops 4000000000 | bytes 12000000 | tf_op jit(solution)/shard_map/front0/pallas_call | solution.py:161
  12.7 8.0 %all-to-all-start = ((f32[16,33,8,128]{3,2,1,0:T(8,128)}), f32[16,33,8,128]{3,2,1,0:T(8,128)S(1)}, u32[]{:S(2)}, u32[]{:S(2)}) async-start(f32[16,33,8,128]{3,2,1,0:T(8,128)} %bitcast.7), calls=%async_computation | async-start | bytes 4325376 | tf_op jit(solution)/shard_map/all_to_all | solution.py:492
  22.0 6.5 %front1.1 = (f32[16,200,128]{2,1,0:T(8,128)S(1)}, f32[16,64,128]{2,1,0:T(8,128)S(1)}) custom-call(f32[2,129]{1,0:T(2,128)S(1)} %copy-done.7, f32[2,4,512,256]{3,2,1,0:T(8,128)} %x_ref.3, f32[2,4,512,128]{3,2,1,0:T(8,128)} %collective-permute-done.h_ref, bf16[2,4,256,256]{3,2,1,0:T(8,128)(2,1)S(1)} %copy-done.9), custom_call_target="tpu_custom_call" | custom-call | flops 4000000000 | bytes 8000000 | tf_op jit(solution)/shard_map/front1/pallas_call | solution.py:185
  29.7 23.0 %all-to-all-done.r_ref = f32[16,33,8,128]{3,2,1,0:T(8,128)S(1)} async-done(((f32[16,33,8,128]{3,2,1,0:T(8,128)}), f32[16,33,8,128]{3,2,1,0:T(8,128)S(1)}, u32[]{:S(2)}, u32[]{:S(2)}) %all-to-all-start) | async-done | bytes 2162720 | tf_op jit(solution)/shard_map/all_to_all | solution.py:492
  54.0 7.1 %all-to-all-start.1 = ((f32[16,200,128]{2,1,0:T(8,128)}), f32[16,200,128]{2,1,0:T(8,128)S(1)}, u32[]{:S(2)}, u32[]{:S(2)}) async-start(f32[16,200,128]{2,1,0:T(8,128)} %copy-done.5), calls=%async_computation.1 | async-start | bytes 3276800 | tf_op jit(solution)/shard_map/all_to_all | solution.py:492
  62.9 7.0 %gram0.1 = (f32[32,128,128]{2,1,0:T(8,128)S(1)}, bf16[2,32,64,256]{3,2,1,0:T(8,128)(2,1)}) custom-call(s32[32,2]{1,0:T(8,128)S(1)} %copy.11.mask_ref, f32[16,33,8,128]{3,2,1,0:T(8,128)S(1)} %copy-done.3), custom_call_target="tpu_custom_call" | custom-call | flops 2000000000 | bytes 6000000 | tf_op jit(solution)/shard_map/gram0/pallas_call | solution.py:270
  71.2 14.8 %all-to-all-done.1 = f32[16,200,128]{2,1,0:T(8,128)S(1)} async-done(((f32[16,200,128]{2,1,0:T(8,128)}), f32[16,200,128]{2,1,0:T(8,128)S(1)}, u32[]{:S(2)}, u32[]{:S(2)}) %all-to-all-start.1) | async-done | bytes 1638432 | tf_op jit(solution)/shard_map/all_to_all | solution.py:492
  87.6 6.0 %gram_a.1 = (f32[12,128,128]{2,1,0:T(8,128)S(1)}, f32[12,128,128]{2,1,0:T(8,128)S(1)}, bf16[2,32,64,256]{3,2,1,0:T(8,128)(2,1)}) custom-call(s32[2]{0:T(128)S(1)} %pad_add_fusion.spot_ref, s32[32,2]{1,0:T(8,128)S(1)} %copy.11.mask_ref, f32[32,128,128]{2,1,0:T(8,128)S(1)} %copy-done.1, ...), custom_call_target="tpu_custom_call", output_to_operand_aliasing={{2}: (4, {})} | custom-call | flops 1500000000 | bytes 4500000 | tf_op jit(solution)/shard_map/gram_a/pallas_call | solution.py:323
  93.6 15.7 %all_to_all.15 = f32[16,64,128]{2,1,0:T(8,128)S(1)} all-to-all(f32[16,64,128]{2,1,0:T(8,128)S(1)} %get-tuple-element.26), channel_id=1, replica_groups=mesh['range'=8,'chan'=16] {'chan'}, dimensions={0} | all-to-all | bytes 1048576 | tf_op jit(solution)/shard_map/all_to_all | solution.py:492
  109.3 2.8 %gram_b.1 = (f32[4,128,128]{2,1,0:T(8,128)S(1)}, f32[4,128,128]{2,1,0:T(8,128)S(1)}, bf16[2,32,64,256]{3,2,1,0:T(8,128)(2,1)}) custom-call(s32[2]{0:T(128)S(1)} %pad_add_fusion.spot_ref, s32[32,2]{1,0:T(8,128)S(1)} %copy.11.mask_ref, f32[32,128,128]{2,1,0:T(8,128)S(1)} %copy-done.1, f32[16,25,8,128]{3,2,1,0:T(8,128)S(1)} %bitcast.6, ...), custom_call_target="tpu_custom_call", output_to_operand_aliasing={{2}: (5, {})} | custom-call | flops 500000000 | bytes 1500000 | tf_op jit(solution)/shard_map/gram_b/pallas_call | solution.py:323
  112.8 4.6 %collective-permute-start.14 = (f32[3,128,128]{2,1,0:T(8,128)S(1)}, f32[3,128,128]{2,1,0:T(8,128)S(1)}, u32[]{:S(2)}, u32[]{:S(2)}) collective-permute-start(f32[3,128,128]{2,1,0:T(8,128)S(1)} %get-tuple-element.40), channel_id=1, source_target_pairs={{0,64},{16,80},{32,96},{48,112},{64,0},{80,16},{96,32},{112,48},{1... | collective-permute-start | bytes 589832 | tf_op jit(solution)/shard_map/ppermute | solution.py:484
  118.0 2.1 %collective-permute-start.2 = (f32[1,128,128]{2,1,0:T(8,128)S(1)}, f32[1,128,128]{2,1,0:T(8,128)S(1)}, u32[]{:S(2)}, u32[]{:S(2)}) collective-permute-start(f32[1,128,128]{2,1,0:T(8,128)S(1)} %get-tuple-element.33), channel_id=1, source_target_pairs={{0,32},{16,48},{32,64},{48,80},{64,96},{80,112},{96,0},{112,16},{1... | collective-permute-start | bytes 196616 | tf_op jit(solution)/shard_map/ppermute | solution.py:484
  121.5 2.1 %collective-permute-start.4 = (f32[1,128,128]{2,1,0:T(8,128)S(1)}, f32[1,128,128]{2,1,0:T(8,128)S(1)}, u32[]{:S(2)}, u32[]{:S(2)}) collective-permute-start(f32[1,128,128]{2,1,0:T(8,128)S(1)} %get-tuple-element.35), channel_id=1, source_target_pairs={{0,96},{16,112},{32,0},{48,16},{64,32},{80,48},{96,64},{112,80},{1... | collective-permute-start | bytes 196616 | tf_op jit(solution)/shard_map/ppermute | solution.py:484
  123.7 3.7 %collective-permute-done.14.refs_2_ = f32[3,128,128]{2,1,0:T(8,128)S(1)} collective-permute-done((f32[3,128,128]{2,1,0:T(8,128)S(1)}, f32[3,128,128]{2,1,0:T(8,128)S(1)}, u32[]{:S(2)}, u32[]{:S(2)}) %collective-permute-start.14) | collective-permute-done | bytes 196640 | tf_op jit(solution)/shard_map/ppermute | solution.py:484
  127.4 15.6 %factor.3.refs_0_ = f32[3,128,128]{2,1,0:T(8,128)S(1)} custom-call(f32[3,128,128]{2,1,0:T(8,128)S(1)} %get-tuple-element.38.refs_0_, f32[3,128,128]{2,1,0:T(8,128)S(1)} %collective-permute-done.13.refs_1_, f32[3,128,128]{2,1,0:T(8,128)S(1)} %collective-permute-done.14.refs_2_, f32[3,128,128]{2,1,0:T(8,128)S(1)} %collective-permute-done.15.refs_3_), custom_call_target="tpu_custom_call" | custom-call | flops 8000000000 | bytes 2000000 | tf_op jit(solution)/shard_map/factor/pallas_call | solution.py:432
  143.0 2.3 %collective-permute-start.18 = (f32[3,128,128]{2,1,0:T(8,128)S(1)}, f32[3,128,128]{2,1,0:T(8,128)S(1)}, u32[]{:S(2)}, u32[]{:S(2)}) collective-permute-start(f32[3,128,128]{2,1,0:T(8,128)S(1)} %factor.3.refs_0_), channel_id=1, source_target_pairs={{0,96},{16,112},{32,0},{48,16},{64,32},{80,48},{96,64},{112,80},{1... | collective-permute-start | bytes 589832 | tf_op jit(solution)/shard_map/ppermute | solution.py:484
  146.2 13.0 %factor.2.refs_0_ = f32[1,128,128]{2,1,0:T(8,128)S(1)} custom-call(f32[1,128,128]{2,1,0:T(8,128)S(1)} %get-tuple-element.32.refs_0_, f32[1,128,128]{2,1,0:T(8,128)S(1)} %collective-permute-done.2.refs_1_, f32[1,128,128]{2,1,0:T(8,128)S(1)} %collective-permute-done.3.refs_2_, f32[1,128,128]{2,1,0:T(8,128)S(1)} %collective-permute-done.4.refs_3_), custom_call_target="tpu_custom_call" | custom-call | flops 8000000000 | bytes 2000000 | tf_op jit(solution)/shard_map/factor/pallas_call | solution.py:432
  159.2 2.4 %collective-permute-start.7 = (f32[1,128,128]{2,1,0:T(8,128)S(1)}, f32[1,128,128]{2,1,0:T(8,128)S(1)}, u32[]{:S(2)}, u32[]{:S(2)}) collective-permute-start(f32[1,128,128]{2,1,0:T(8,128)S(1)} %factor.2.refs_0_), channel_id=1, source_target_pairs={{0,96},{16,112},{32,0},{48,16},{64,32},{80,48},{96,64},{112,80},{1... | collective-permute-start | bytes 196616 | tf_op jit(solution)/shard_map/ppermute | solution.py:484
  162.2 1.9 %collective-permute-done.7.refs_3_ = f32[1,128,128]{2,1,0:T(8,128)S(1)} collective-permute-done((f32[1,128,128]{2,1,0:T(8,128)S(1)}, f32[1,128,128]{2,1,0:T(8,128)S(1)}, u32[]{:S(2)}, u32[]{:S(2)}) %collective-permute-start.7) | collective-permute-done | bytes 65568 | tf_op jit(solution)/shard_map/ppermute | solution.py:484
  164.1 2.5 %collective-permute-start.6 = (f32[1,128,128]{2,1,0:T(8,128)S(1)}, f32[1,128,128]{2,1,0:T(8,128)S(1)}, u32[]{:S(2)}, u32[]{:S(2)}) collective-permute-start(f32[1,128,128]{2,1,0:T(8,128)S(1)} %factor.2.refs_0_), channel_id=1, source_target_pairs={{0,64},{16,80},{32,96},{48,112},{64,0},{80,16},{96,32},{112,48},{1... | collective-permute-start | bytes 196616 | tf_op jit(solution)/shard_map/ppermute | solution.py:484
  166.6 3.3 %collective-permute-done.6.refs_2_ = f32[1,128,128]{2,1,0:T(8,128)S(1)} collective-permute-done((f32[1,128,128]{2,1,0:T(8,128)S(1)}, f32[1,128,128]{2,1,0:T(8,128)S(1)}, u32[]{:S(2)}, u32[]{:S(2)}) %collective-permute-start.6) | collective-permute-done | bytes 65568 | tf_op jit(solution)/shard_map/ppermute | solution.py:484
  169.8 2.0 %collective-permute-start.5 = (f32[1,128,128]{2,1,0:T(8,128)S(1)}, f32[1,128,128]{2,1,0:T(8,128)S(1)}, u32[]{:S(2)}, u32[]{:S(2)}) collective-permute-start(f32[1,128,128]{2,1,0:T(8,128)S(1)} %factor.2.refs_0_), channel_id=1, source_target_pairs={{0,32},{16,48},{32,64},{48,80},{64,96},{80,112},{96,0},{112,16},{1... | collective-permute-start | bytes 196616 | tf_op jit(solution)/shard_map/ppermute | solution.py:484
  171.8 3.5 %collective-permute-done.5.refs_1_ = f32[1,128,128]{2,1,0:T(8,128)S(1)} collective-permute-done((f32[1,128,128]{2,1,0:T(8,128)S(1)}, f32[1,128,128]{2,1,0:T(8,128)S(1)}, u32[]{:S(2)}, u32[]{:S(2)}) %collective-permute-start.5) | collective-permute-done | bytes 65568 | tf_op jit(solution)/shard_map/ppermute | solution.py:484
  176.3 2.8 %unpack.2.refs_8_ = f32[32,2,128,128]{3,2,1,0:T(8,128)} custom-call(s32[2]{0:T(128)S(1)} %pad_add_fusion.spot_ref, f32[3,128,128]{2,1,0:T(8,128)S(1)} %factor.3.refs_0_, f32[3,128,128]{2,1,0:T(8,128)S(1)} %collective-permute-done.16.refs_1_, f32[3,128,128]{2,1,0:T(8,128)S(1)} %collective-permute-done.17.refs_2_, ...), custom_call_target="tpu_custom_call" | custom-call | flops 1000000 | bytes 4800000 | tf_op jit(solution)/shard_map/unpack/pallas_call | solution.py:470
  (62 shorter events, 20.0 us)
Async XLA Ops:
  11.4 9.3 %collective-permute-start = (f32[2,4,512,128]{3,2,1,0:T(8,128)}, f32[2,4,512,128]{3,2,1,0:T(8,128)}, u32[]{:S(2)}, u32[]{:S(2)}) collective-permute-start(f32[2,4,512,128]{3,2,1,0:T(8,128)} %get-tuple-element.24), channel_id=1, source_target_pairs={{16,0},{32,16},{48,32},{64,48},{80,64},{96,80},{112,96},{17,1},{33... | collective-permute-start | bytes 6291464 | tf_op jit(solution)/shard_map/ppermute | solution.py:510
  12.7 40.0 %all-to-all-start = ((f32[16,33,8,128]{3,2,1,0:T(8,128)}), f32[16,33,8,128]{3,2,1,0:T(8,128)S(1)}, u32[]{:S(2)}, u32[]{:S(2)}) async-start(f32[16,33,8,128]{3,2,1,0:T(8,128)} %bitcast.7), calls=%async_computation | async-start | bytes 4325376 | tf_op jit(solution)/shard_map/all_to_all | solution.py:492
  54.0 31.9 %all-to-all-start.1 = ((f32[16,200,128]{2,1,0:T(8,128)}), f32[16,200,128]{2,1,0:T(8,128)S(1)}, u32[]{:S(2)}, u32[]{:S(2)}) async-start(f32[16,200,128]{2,1,0:T(8,128)} %copy-done.5), calls=%async_computation.1 | async-start | bytes 3276800 | tf_op jit(solution)/shard_map/all_to_all | solution.py:492
  93.6 18.5 %collective-permute-start.12 = (f32[12,128,128]{2,1,0:T(8,128)S(1)}, f32[12,128,128]{2,1,0:T(8,128)S(1)}, u32[]{:S(2)}, u32[]{:S(2)}) collective-permute-start(f32[12,128,128]{2,1,0:T(8,128)S(1)} %get-tuple-element.37), channel_id=1, source_target_pairs={{0,16},{16,0},{32,48},{48,32},{64,80},{80,64},{96,112},{112,96},{1... | collective-permute-start | bytes 2359304 | tf_op jit(solution)/shard_map/ppermute | solution.py:488
  112.1 5.3 %collective-permute-start.1 = (f32[4,128,128]{2,1,0:T(8,128)S(1)}, f32[4,128,128]{2,1,0:T(8,128)S(1)}, u32[]{:S(2)}, u32[]{:S(2)}) collective-permute-start(f32[4,128,128]{2,1,0:T(8,128)S(1)} %get-tuple-element.31), channel_id=1, source_target_pairs={{0,16},{16,0},{32,48},{48,32},{64,80},{80,64},{96,112},{112,96},{1... | collective-permute-start | bytes 786440 | tf_op jit(solution)/shard_map/ppermute | solution.py:488
  112.8 8.8 %collective-permute-start.13 = (f32[3,128,128]{2,1,0:T(8,128)S(1)}, f32[3,128,128]{2,1,0:T(8,128)S(1)}, u32[]{:S(2)}, u32[]{:S(2)}) collective-permute-start(f32[3,128,128]{2,1,0:T(8,128)S(1)} %get-tuple-element.39), channel_id=1, source_target_pairs={{0,32},{16,48},{32,64},{48,80},{64,96},{80,112},{96,0},{112,16},{1... | collective-permute-start | bytes 589832 | tf_op jit(solution)/shard_map/ppermute | solution.py:484
  112.8 14.5 %collective-permute-start.14 = (f32[3,128,128]{2,1,0:T(8,128)S(1)}, f32[3,128,128]{2,1,0:T(8,128)S(1)}, u32[]{:S(2)}, u32[]{:S(2)}) collective-permute-start(f32[3,128,128]{2,1,0:T(8,128)S(1)} %get-tuple-element.40), channel_id=1, source_target_pairs={{0,64},{16,80},{32,96},{48,112},{64,0},{80,16},{96,32},{112,48},{1... | collective-permute-start | bytes 589832 | tf_op jit(solution)/shard_map/ppermute | solution.py:484
  117.4 9.9 %collective-permute-start.15 = (f32[3,128,128]{2,1,0:T(8,128)S(1)}, f32[3,128,128]{2,1,0:T(8,128)S(1)}, u32[]{:S(2)}, u32[]{:S(2)}) collective-permute-start(f32[3,128,128]{2,1,0:T(8,128)S(1)} %get-tuple-element.41), channel_id=1, source_target_pairs={{0,96},{16,112},{32,0},{48,16},{64,32},{80,48},{96,64},{112,80},{1... | collective-permute-start | bytes 589832 | tf_op jit(solution)/shard_map/ppermute | solution.py:484
  118.0 27.2 %collective-permute-start.2 = (f32[1,128,128]{2,1,0:T(8,128)S(1)}, f32[1,128,128]{2,1,0:T(8,128)S(1)}, u32[]{:S(2)}, u32[]{:S(2)}) collective-permute-start(f32[1,128,128]{2,1,0:T(8,128)S(1)} %get-tuple-element.33), channel_id=1, source_target_pairs={{0,32},{16,48},{32,64},{48,80},{64,96},{80,112},{96,0},{112,16},{1... | collective-permute-start | bytes 196616 | tf_op jit(solution)/shard_map/ppermute | solution.py:484
  120.1 26.1 %collective-permute-start.3 = (f32[1,128,128]{2,1,0:T(8,128)S(1)}, f32[1,128,128]{2,1,0:T(8,128)S(1)}, u32[]{:S(2)}, u32[]{:S(2)}) collective-permute-start(f32[1,128,128]{2,1,0:T(8,128)S(1)} %get-tuple-element.34), channel_id=1, source_target_pairs={{0,64},{16,80},{32,96},{48,112},{64,0},{80,16},{96,32},{112,48},{1... | collective-permute-start | bytes 196616 | tf_op jit(solution)/shard_map/ppermute | solution.py:484
  121.5 24.7 %collective-permute-start.4 = (f32[1,128,128]{2,1,0:T(8,128)S(1)}, f32[1,128,128]{2,1,0:T(8,128)S(1)}, u32[]{:S(2)}, u32[]{:S(2)}) collective-permute-start(f32[1,128,128]{2,1,0:T(8,128)S(1)} %get-tuple-element.35), channel_id=1, source_target_pairs={{0,96},{16,112},{32,0},{48,16},{64,32},{80,48},{96,64},{112,80},{1... | collective-permute-start | bytes 196616 | tf_op jit(solution)/shard_map/ppermute | solution.py:484
  143.0 18.6 %collective-permute-start.18 = (f32[3,128,128]{2,1,0:T(8,128)S(1)}, f32[3,128,128]{2,1,0:T(8,128)S(1)}, u32[]{:S(2)}, u32[]{:S(2)}) collective-permute-start(f32[3,128,128]{2,1,0:T(8,128)S(1)} %factor.3.refs_0_), channel_id=1, source_target_pairs={{0,96},{16,112},{32,0},{48,16},{64,32},{80,48},{96,64},{112,80},{1... | collective-permute-start | bytes 589832 | tf_op jit(solution)/shard_map/ppermute | solution.py:484
  145.3 16.8 %collective-permute-start.17 = (f32[3,128,128]{2,1,0:T(8,128)S(1)}, f32[3,128,128]{2,1,0:T(8,128)S(1)}, u32[]{:S(2)}, u32[]{:S(2)}) collective-permute-start(f32[3,128,128]{2,1,0:T(8,128)S(1)} %factor.3.refs_0_), channel_id=1, source_target_pairs={{0,64},{16,80},{32,96},{48,112},{64,0},{80,16},{96,32},{112,48},{1... | collective-permute-start | bytes 589832 | tf_op jit(solution)/shard_map/ppermute | solution.py:484
  145.3 21.3 %collective-permute-start.16 = (f32[3,128,128]{2,1,0:T(8,128)S(1)}, f32[3,128,128]{2,1,0:T(8,128)S(1)}, u32[]{:S(2)}, u32[]{:S(2)}) collective-permute-start(f32[3,128,128]{2,1,0:T(8,128)S(1)} %factor.3.refs_0_), channel_id=1, source_target_pairs={{0,32},{16,48},{32,64},{48,80},{64,96},{80,112},{96,0},{112,16},{1... | collective-permute-start | bytes 589832 | tf_op jit(solution)/shard_map/ppermute | solution.py:484
  159.2 4.9 %collective-permute-start.7 = (f32[1,128,128]{2,1,0:T(8,128)S(1)}, f32[1,128,128]{2,1,0:T(8,128)S(1)}, u32[]{:S(2)}, u32[]{:S(2)}) collective-permute-start(f32[1,128,128]{2,1,0:T(8,128)S(1)} %factor.2.refs_0_), channel_id=1, source_target_pairs={{0,96},{16,112},{32,0},{48,16},{64,32},{80,48},{96,64},{112,80},{1... | collective-permute-start | bytes 196616 | tf_op jit(solution)/shard_map/ppermute | solution.py:484
  161.6 13.7 %collective-permute-start.19 = (f32[3,128,128]{2,1,0:T(8,128)S(1)}, f32[3,128,128]{2,1,0:T(8,128)S(1)}, u32[]{:S(2)}, u32[]{:S(2)}) collective-permute-start(f32[3,128,128]{2,1,0:T(8,128)S(1)} %factor.3.refs_0_), channel_id=1, source_target_pairs={{0,16},{16,0},{32,48},{48,32},{64,80},{80,64},{96,112},{112,96},{1... | collective-permute-start | bytes 589832 | tf_op jit(solution)/shard_map/ppermute | solution.py:488
  161.6 14.3 %collective-permute-start.22 = (f32[3,128,128]{2,1,0:T(8,128)S(1)}, f32[3,128,128]{2,1,0:T(8,128)S(1)}, u32[]{:S(2)}, u32[]{:S(2)}) collective-permute-start(f32[3,128,128]{2,1,0:T(8,128)S(1)} %collective-permute-done.18.refs_3_), channel_id=1, source_target_pairs={{0,16},{16,0},{32,48},{48,32},{64,80},{80,64},{96,112},{112,96},{1... | collective-permute-start | bytes 589832 | tf_op jit(solution)/shard_map/ppermute | solution.py:488
  162.1 13.8 %collective-permute-start.21 = (f32[3,128,128]{2,1,0:T(8,128)S(1)}, f32[3,128,128]{2,1,0:T(8,128)S(1)}, u32[]{:S(2)}, u32[]{:S(2)}) collective-permute-start(f32[3,128,128]{2,1,0:T(8,128)S(1)} %collective-permute-done.17.refs_2_), channel_id=1, source_target_pairs={{0,16},{16,0},{32,48},{48,32},{64,80},{80,64},{96,112},{112,96},{1... | collective-permute-start | bytes 589832 | tf_op jit(solution)/shard_map/ppermute | solution.py:488
  164.1 5.8 %collective-permute-start.6 = (f32[1,128,128]{2,1,0:T(8,128)S(1)}, f32[1,128,128]{2,1,0:T(8,128)S(1)}, u32[]{:S(2)}, u32[]{:S(2)}) collective-permute-start(f32[1,128,128]{2,1,0:T(8,128)S(1)} %factor.2.refs_0_), channel_id=1, source_target_pairs={{0,64},{16,80},{32,96},{48,112},{64,0},{80,16},{96,32},{112,48},{1... | collective-permute-start | bytes 196616 | tf_op jit(solution)/shard_map/ppermute | solution.py:484
  166.5 9.8 %collective-permute-start.20 = (f32[3,128,128]{2,1,0:T(8,128)S(1)}, f32[3,128,128]{2,1,0:T(8,128)S(1)}, u32[]{:S(2)}, u32[]{:S(2)}) collective-permute-start(f32[3,128,128]{2,1,0:T(8,128)S(1)} %collective-permute-done.16.refs_1_), channel_id=1, source_target_pairs={{0,16},{16,0},{32,48},{48,32},{64,80},{80,64},{96,112},{112,96},{1... | collective-permute-start | bytes 589832 | tf_op jit(solution)/shard_map/ppermute | solution.py:488
  169.8 5.5 %collective-permute-start.5 = (f32[1,128,128]{2,1,0:T(8,128)S(1)}, f32[1,128,128]{2,1,0:T(8,128)S(1)}, u32[]{:S(2)}, u32[]{:S(2)}) collective-permute-start(f32[1,128,128]{2,1,0:T(8,128)S(1)} %factor.2.refs_0_), channel_id=1, source_target_pairs={{0,32},{16,48},{32,64},{48,80},{64,96},{80,112},{96,0},{112,16},{1... | collective-permute-start | bytes 196616 | tf_op jit(solution)/shard_map/ppermute | solution.py:484
  175.3 3.8 %collective-permute-start.8 = (f32[1,128,128]{2,1,0:T(8,128)S(1)}, f32[1,128,128]{2,1,0:T(8,128)S(1)}, u32[]{:S(2)}, u32[]{:S(2)}) collective-permute-start(f32[1,128,128]{2,1,0:T(8,128)S(1)} %factor.2.refs_0_), channel_id=1, source_target_pairs={{0,16},{16,0},{32,48},{48,32},{64,80},{80,64},{96,112},{112,96},{1... | collective-permute-start | bytes 196616 | tf_op jit(solution)/shard_map/ppermute | solution.py:488
  175.3 3.8 %collective-permute-start.11 = (f32[1,128,128]{2,1,0:T(8,128)S(1)}, f32[1,128,128]{2,1,0:T(8,128)S(1)}, u32[]{:S(2)}, u32[]{:S(2)}) collective-permute-start(f32[1,128,128]{2,1,0:T(8,128)S(1)} %collective-permute-done.7.refs_3_), channel_id=1, source_target_pairs={{0,16},{16,0},{32,48},{48,32},{64,80},{80,64},{96,112},{112,96},{1... | collective-permute-start | bytes 196616 | tf_op jit(solution)/shard_map/ppermute | solution.py:488
  175.8 3.3 %collective-permute-start.10 = (f32[1,128,128]{2,1,0:T(8,128)S(1)}, f32[1,128,128]{2,1,0:T(8,128)S(1)}, u32[]{:S(2)}, u32[]{:S(2)}) collective-permute-start(f32[1,128,128]{2,1,0:T(8,128)S(1)} %collective-permute-done.6.refs_2_), channel_id=1, source_target_pairs={{0,16},{16,0},{32,48},{48,32},{64,80},{80,64},{96,112},{112,96},{1... | collective-permute-start | bytes 196616 | tf_op jit(solution)/shard_map/ppermute | solution.py:488
  (12 other events, 54.2 us)

commit v2 on v1

--- a/solution.py
+++ b/solution.py
@@ -12,12 +12,11 @@
 PULSES = 512
 TILE = 128
 BINS = 32
+GROUP = 8
 WIDE = BINS + 1
 CHANS = 16
 LOCAL = 4
-LATE = 8
-EARLY = BINS - LATE
-STRIP = 16
+STRIP = 32
 F32 = jnp.float32
 BF16 = jnp.bfloat16
 VMEM = pl.BlockSpec(memory_space=pltpu.VMEM)
@@ -25,7 +24,7 @@
 ANY = pl.BlockSpec(memory_space=pl.ANY)
 
 
-def params(mib=48):
+def params(mib=60):
     return pltpu.CompilerParams(vmem_limit_bytes=mib << 20)
 
 
@@ -131,7 +130,7 @@
         add_edges(out_ref)
 
 
-def front1_kernel(chirp_ref, x_ref, h_ref, w_ref, a_ref, b_ref, pad_ref, kmat_ref, flat_ref):
+def front1_kernel(chirp_ref, x_ref, h_ref, w_ref, out_ref, pad_ref, kmat_ref):
     step = pl.program_id(0)
 
     @pl.when(step == 0)
@@ -141,16 +140,11 @@
     windows = []
     for c in range(2):
         windows.append(jnp.concatenate([x_ref[0, c], h_ref[0, c], x_ref[1, c], h_ref[1, c]], 1))
-    front_body(step, windows, kmat_ref, w_ref, store_into(flat_ref, step))
+    front_body(step, windows, kmat_ref, w_ref, store_into(out_ref, step))
 
     @pl.when(step == 1)
     def _():
-        add_edges(flat_ref)
-        for k in range(CHANS):
-            base = k * WIDE * 8
-            middle = (EARLY + 1) * 8
-            a_ref[k] = flat_ref[pl.ds(base, middle), :]
-            b_ref[k] = flat_ref[pl.ds(base + middle, LATE * 8), :]
+        add_edges(out_ref)
 
 
 def front_scratch():
@@ -191,15 +185,9 @@
             pl.BlockSpec((2, 2, PULSES, TILE), lambda i: (0, i, 0, 0)),
             pl.BlockSpec(w.shape, lambda i: (0, 0, 0, 0)),
         ],
-        out_specs=[
-            pl.BlockSpec((CHANS, (EARLY + 1) * 8, TILE), lambda i: (0, 0, 0)),
-            pl.BlockSpec((CHANS, LATE * 8, TILE), lambda i: (0, 0, 0)),
-        ],
-        out_shape=[
-            jax.ShapeDtypeStruct((CHANS, (EARLY + 1) * 8, TILE), F32),
-            jax.ShapeDtypeStruct((CHANS, LATE * 8, TILE), F32),
-        ],
-        scratch_shapes=front_scratch() + [pltpu.VMEM((CHANS * WIDE * 8, TILE), F32)],
+        out_specs=pl.BlockSpec((CHANS * WIDE * 8, TILE), lambda i: (0, 0)),
+        out_shape=jax.ShapeDtypeStruct((CHANS * WIDE * 8, TILE), F32),
+        scratch_shapes=front_scratch(),
         compiler_params=params(),
         cost_estimate=cost(4e9, 8e6),
         name="front1",
@@ -241,107 +229,106 @@
     return jnp.where(row <= column, both[:, :128], both[:, 128:])
 
 
-def gram0_kernel(mask_ref, r_ref, sums_ref, spectra_ref, high_ref, low_ref):
-    def plant_one(b, carry):
-        def store(rh, ih):
-            @pl.when(b < BINS)
-            def _():
-                spectra_ref[0, b] = rh
-                spectra_ref[1, b] = ih
-
-        plant(b, r_ref[:, b], store, high_ref, low_ref)
-        return carry
-
-    lax.fori_loop(0, WIDE, plant_one, 0, unroll=3)
-
-    def one(b, carry):
-        weight = mask_ref[b, 0].astype(F32)
-        sums_ref[b] = bin_gram(b, high_ref, low_ref) * weight
-        return carry
-
-    lax.fori_loop(0, BINS, one, 0, unroll=4)
-
-
 def gram_scratch(count):
     return [pltpu.VMEM((2, count + 1, 64, 2 * TILE), BF16)] * 2
 
 
+def plant_all(r_ref, edge_ref, spectra_ref, high_ref, low_ref):
+    for b in range(GROUP):
+
+        def store(rh, ih, b=b):
+            spectra_ref[0, b] = rh
+            spectra_ref[1, b] = ih
+
+        plant(b, r_ref[:, b], store, high_ref, low_ref)
+    plant(GROUP, edge_ref[:, 0], lambda rh, ih: None, high_ref, low_ref)
+
+
+def gram0_kernel(mask_ref, r_ref, edge_ref, sums_ref, spectra_ref, high_ref, low_ref):
+    first = pl.program_id(0) * GROUP
+    plant_all(r_ref, edge_ref, spectra_ref, high_ref, low_ref)
+    for b in range(GROUP):
+        weight = mask_ref[0, first + b].astype(F32)
+        sums_ref[b] = bin_gram(b, high_ref, low_ref) * weight
+
+
 def gram0(mask, received):
     return pl.pallas_call(
         gram0_kernel,
-        in_specs=[SMEM, VMEM],
+        grid=(BINS // GROUP,),
+        in_specs=[
+            SMEM,
+            pl.BlockSpec((CHANS, GROUP, 8, TILE), lambda i: (0, i, 0, 0)),
+            pl.BlockSpec((CHANS, 1, 8, TILE), lambda i: (0, GROUP * (i + 1), 0, 0)),
+        ],
         out_specs=[
-            VMEM,
-            pl.BlockSpec((2, BINS, 64, TILE), lambda i: (0, 0, 0, 0)),
-        ],
-        grid=(1,),
+            pl.BlockSpec((GROUP, 128, 128), lambda i: (i, 0, 0)),
+            pl.BlockSpec((2, GROUP, 64, TILE), lambda i: (0, i, 0, 0)),
+        ],
         out_shape=[
             jax.ShapeDtypeStruct((BINS, 128, 128), F32),
             jax.ShapeDtypeStruct((2, BINS, 64, 2 * TILE), BF16),
         ],
-        scratch_shapes=gram_scratch(BINS),
-        compiler_params=params(),
+        scratch_shapes=gram_scratch(GROUP),
+        compiler_params=params(20),
         cost_estimate=cost(2e9, 6e6),
         name="gram0",
-    )(mask, received)
-
-
-def gram1_kernel(first, count, split_at, spot_ref, mask_ref, sums_ref, *refs):
-    pieces = refs[: len(split_at)]
-    _, keep_ref, send_ref, spectra_ref, high_ref, low_ref = refs[len(split_at) :]
-    place = 0
-    for piece, (start, amount) in zip(pieces, split_at):
-
-        def plant_one(i, carry, piece=piece, start=start, place=place):
-            def store(rh, ih):
-                @pl.when(place + i < count)
-                def _():
-                    spectra_ref[0, place + i] = rh
-                    spectra_ref[1, place + i] = ih
-
-            plant(place + i, piece[:, start + i], store, high_ref, low_ref)
-            return carry
-
-        lax.fori_loop(0, amount, plant_one, 0, unroll=min(amount, 4))
-        place += amount
-    half = count // 2
-    core = spot_ref[1]
-    for out_ref, base in ((send_ref, (1 - core) * half), (keep_ref, core * half)):
-
-        def one(i, carry, out_ref=out_ref, base=base):
-            b = base + i
-            weight = mask_ref[first + b, 1].astype(F32)
-            out_ref[i] = sums_ref[b] + bin_gram(b, high_ref, low_ref) * weight
-            return carry
-
-        lax.fori_loop(0, half, one, 0, unroll=4)
-
-
-def gram1(first, count, spot, mask, sums, pieces, split_at, spectra, name):
-    half = count // 2
-    block = first // count
-    return pl.pallas_call(
-        functools.partial(gram1_kernel, first, count, split_at),
-        grid=(1,),
-        in_specs=[
-            SMEM,
-            SMEM,
-            pl.BlockSpec((count, 128, 128), lambda i: (block, 0, 0)),
-        ]
-        + [VMEM] * len(pieces)
-        + [ANY],
-        out_specs=[VMEM, VMEM, pl.BlockSpec((2, count, 64, TILE), lambda i: (0, block, 0, 1))],
-        out_shape=[
-            jax.ShapeDtypeStruct((half, 128, 128), F32),
-            jax.ShapeDtypeStruct((half, 128, 128), F32),
-            jax.ShapeDtypeStruct(spectra.shape, spectra.dtype),
-        ],
-        scratch_shapes=gram_scratch(count),
-        input_output_aliases={3 + len(pieces): 2},
-        compiler_params=params(),
-        cost_estimate=cost(2e9 * count / 32, 6e6 * count / 32),
-        name=name,
-    )(spot, mask, sums, *pieces, spectra)
+    )(mask, received, received)
+
+
+def gram1_kernel(spot_ref, mask_ref, r_ref, edge_ref, sums_ref, _, send_ref, keep_ref, spectra_ref, high_ref, low_ref):
+    steps = BINS // GROUP
+    step = pl.program_id(0)
+    first = lax.rem(step + (1 - spot_ref[1]) * (steps // 2), steps) * GROUP
+    plant_all(r_ref, edge_ref, spectra_ref, high_ref, low_ref)
+
+    def fill(out_ref):
+        for b in range(GROUP):
+            weight = mask_ref[1, first + b].astype(F32)
+            out_ref[b] = sums_ref[b] + bin_gram(b, high_ref, low_ref) * weight
+
+    @pl.when(step < steps // 2)
+    def _():
+        fill(send_ref)
+
+    @pl.when(step >= steps // 2)
+    def _():
+        fill(keep_ref)
+
+
+def gram1(spot, mask, received, sums, spectra):
+    steps = BINS // GROUP
+    half = steps // 2
+
+    def at(i, spot):
+        return lax.rem(i + (1 - spot[1]) * half, steps)
+
+    return pl.pallas_call(
+        gram1_kernel,
+        grid_spec=pltpu.PrefetchScalarGridSpec(
+            num_scalar_prefetch=1,
+            grid=(steps,),
+            in_specs=[
+                SMEM,
+                pl.BlockSpec((CHANS, GROUP, 8, TILE), lambda i, spot: (0, at(i, spot), 0, 0)),
+                pl.BlockSpec((CHANS, 1, 8, TILE), lambda i, spot: (0, GROUP * (at(i, spot) + 1), 0, 0)),
+                pl.BlockSpec((GROUP, 128, 128), lambda i, spot: (at(i, spot), 0, 0)),
+                ANY,
+            ],
+            out_specs=[
+                pl.BlockSpec((GROUP, 128, 128), lambda i, spot: (jnp.minimum(i, half - 1), 0, 0)),
+                pl.BlockSpec((GROUP, 128, 128), lambda i, spot: (jnp.maximum(i - half, 0), 0, 0)),
+                pl.BlockSpec((2, GROUP, 64, TILE), lambda i, spot: (0, at(i, spot), 0, 1)),
+            ],
+            scratch_shapes=gram_scratch(GROUP),
+        ),
+        out_shape=[jax.ShapeDtypeStruct((BINS // 2, 128, 128), F32)] * 2
+        + [jax.ShapeDtypeStruct(spectra.shape, spectra.dtype)],
+        input_output_aliases={5: 2},
+        compiler_params=params(20),
+        cost_estimate=cost(2e9, 6e6),
+        name="gram1",
+    )(spot, mask, received, received, sums, spectra)
 
 
 def core_sum_kernel(share, spot_ref, keep_ref, got_ref, *outs):
@@ -357,16 +344,76 @@
         in_specs=[SMEM, VMEM, VMEM],
         out_specs=[VMEM] * 4,
         out_shape=[jax.ShapeDtypeStruct((share, 128, 128), F32)] * 4,
-        compiler_params=params(),
-        cost_estimate=cost(1e6, 2e6),
+        compiler_params=params(16),
+        cost_estimate=cost(1e6, 1e5),
         name="core_sum",
     )(spot, keep, got)
 
 
+def spread(value):
+    return jnp.broadcast_to(value, (8, 128))
+
+
+def minus(value, left, right):
+    re, im = value
+    lr, li = left
+    rr, ri = right
+    return re - (lr * rr - li * ri), im - (lr * ri + li * rr)
+
+
+def conj(value):
+    return value[0], -value[1]
+
+
+def four_columns(groups, i, place, store_row, last):
+    columns = [
+        [(spread(re[:, place + v : place + v + 1]), spread(im[:, place + v : place + v + 1])) for re, im in groups]
+        for v in range(4)
+    ]
+    g, r = divmod(i, 8)
+    corner = {}
+    for u in range(4):
+        for v in range(u, 4):
+            re, im = columns[v][g]
+            corner[u, v] = spread(re[r + u : r + u + 1]), spread(im[r + u : r + u + 1])
+    re, im = groups[g]
+    rows = [(spread(re[r + u : r + u + 1]), spread(im[r + u : r + u + 1])) for u in range(4)]
+    inverses, upper = [], {}
+    for t in range(4):
+        inverse = lax.rsqrt(corner[t, t][0])
+        inverses.append(inverse)
+        for v in range(t + 1, 4):
+            upper[t, v] = corner[t, v][0] * inverse, corner[t, v][1] * inverse
+        for u in range(t + 1, 4):
+            for v in range(u, 4):
+                corner[u, v] = minus(corner[u, v], conj(upper[t, u]), upper[t, v])
+    found = []
+    for t in range(4):
+        value = rows[t]
+        for u in range(t):
+            value = minus(value, conj(upper[u, t]), found[u])
+        found.append((value[0] * inverses[t], value[1] * inverses[t]))
+        store_row(place + t, found[t][0][0:1], found[t][1][0:1])
+    if last:
+        return groups
+    later = []
+    for g, value in enumerate(groups):
+        if 8 * g + 8 > i + 4:
+            scaled = []
+            for t in range(4):
+                column = columns[t][g]
+                for u in range(t):
+                    column = minus(column, scaled[u], upper[u, t])
+                scaled.append((column[0] * inverses[t], column[1] * inverses[t]))
+            for t in range(4):
+                value = minus(value, scaled[t], found[t])
+        later.append(value)
+    return later
+
+
 def factor_kernel(scaling, *refs):
-    out_ref = refs[-7]
-    ins = refs[:-7]
-    gre_ref, gim_ref, fre_ref, fim_ref, sre_ref, sim_ref = refs[-6:]
+    out_ref, gre_ref, gim_ref, fre_ref, fim_ref = refs[-5:]
+    ins = refs[:-5]
     count = out_ref.shape[0]
     row = lax.broadcasted_iota(jnp.int32, (128, 128), 0)
     column = lax.broadcasted_iota(jnp.int32, (128, 128), 1)
@@ -378,10 +425,12 @@
         turned = packed.T
         gre_ref[n] = jnp.where(row <= column, packed, turned)
         gim_ref[n] = jnp.where(row < column, -turned, jnp.where(row > column, packed, 0.0))
-    high = lax.Precision.HIGHEST
     dims = (((0,), (0,)), ((), ()))
     dot = functools.partial(
-        lax.dot_general, dimension_numbers=dims, preferred_element_type=F32, precision=high
+        lax.dot_general,
+        dimension_numbers=dims,
+        preferred_element_type=F32,
+        precision=lax.Precision.HIGHEST,
     )
     for offset in range(0, 128, STRIP):
         strips = []
@@ -391,38 +440,27 @@
             if offset:
                 fr, fi = fre_ref[n, :offset], fim_ref[n, :offset]
                 lr, li = fr[:, offset : offset + STRIP], fi[:, offset : offset + STRIP]
-                both = jnp.concatenate([fr, fi], 0)
-                re = re - dot(jnp.concatenate([lr, li], 0), both)
-                im = im - dot(jnp.concatenate([-li, lr], 0), both)
-            strips.append((re, im))
-        for i in range(STRIP):
-            place = offset + i
-            later = []
-            for n, (re, im) in enumerate(strips):
-                col_re = re[:, place : place + 1]
-                col_im = im[:, place : place + 1]
-                pivot = re[i : i + 1, place : place + 1]
-                inverse = lax.rsqrt(pivot)
-                row_re = re[i : i + 1] * inverse
-                row_im = im[i : i + 1] * inverse
-                fre_ref[n, place : place + 1] = row_re
-                fim_ref[n, place : place + 1] = row_im
-                if i + 1 < STRIP:
-                    cr = col_re * inverse
-                    ci = col_im * inverse
-                    re, im = (
-                        re - (cr * row_re - ci * row_im),
-                        im - (cr * row_im + ci * row_re),
-                    )
-                later.append((re, im))
-            strips = later
+                left = jnp.concatenate(
+                    [jnp.concatenate([lr, -li], 1), jnp.concatenate([li, lr], 1)], 0
+                )
+                update = dot(left, jnp.concatenate([fr, fi], 0))
+                re = re - update[:STRIP]
+                im = im - update[STRIP:]
+            strips.append([(re[8 * g : 8 * g + 8], im[8 * g : 8 * g + 8]) for g in range(STRIP // 8)])
+        for i in range(0, STRIP, 4):
+            for n in range(count):
+
+                def store_row(place, re, im, n=n):
+                    fre_ref[n, place : place + 1] = re
+                    fim_ref[n, place : place + 1] = im
+
+                strips[n] = four_columns(strips[n], i, offset + i, store_row, i + 4 == STRIP)
+        r = lax.broadcasted_iota(jnp.int32, (STRIP, 128), 0) + offset
+        c = lax.broadcasted_iota(jnp.int32, (STRIP, 128), 1)
         for n in range(count):
-            fre = fre_ref[n, offset : offset + STRIP]
-            fim = fim_ref[n, offset : offset + STRIP]
-            r = lax.broadcasted_iota(jnp.int32, (STRIP, 128), 0) + offset
-            c = lax.broadcasted_iota(jnp.int32, (STRIP, 128), 1)
-            fre_ref[n, offset : offset + STRIP] = jnp.where(c >= r, fre, 0.0)
-            fim_ref[n, offset : offset + STRIP] = jnp.where(c > r, fim, 0.0)
+            here = slice(offset, offset + STRIP)
+            fre_ref[n, here] = jnp.where(c >= r, fre_ref[n, here], 0.0)
+            fim_ref[n, here] = jnp.where(c > r, fim_ref[n, here], 0.0)
     for n in range(count):
         out_ref[n] = fre_ref[n] + fim_ref[n].T
 
@@ -434,10 +472,9 @@
         in_specs=[VMEM] * len(pieces),
         out_specs=VMEM,
         out_shape=jax.ShapeDtypeStruct((count, 128, 128), F32),
-        scratch_shapes=[pltpu.VMEM((count, 128, 128), F32)] * 4
-        + [pltpu.VMEM((count, STRIP, 128), F32)] * 2,
-        compiler_params=params(),
-        cost_estimate=cost(8e9, 2e6),
+        scratch_shapes=[pltpu.VMEM((count, 128, 128), F32)] * 4,
+        compiler_params=params(16),
+        cost_estimate=cost(1e6, 1e5),
         name="factor",
     )(*pieces)
 
@@ -462,22 +499,17 @@
         lax.fori_loop(0, share, one, 0, unroll=True)
 
 
-def unpack(first, spot, pieces, below):
+def unpack(spot, pieces):
     share = pieces[0].shape[0]
-    count = share * 8
-    block = first // count
-    more = [] if below is None else [below]
     return pl.pallas_call(
         functools.partial(unpack_kernel, share),
-        grid=(1,),
-        in_specs=[SMEM] + [VMEM] * 8 + [ANY] * len(more),
-        out_specs=pl.BlockSpec((count, 2, 128, 128), lambda i: (block, 0, 0, 0)),
+        in_specs=[SMEM] + [VMEM] * 8,
+        out_specs=VMEM,
         out_shape=jax.ShapeDtypeStruct((BINS, 2, 128, 128), F32),
-        input_output_aliases={9: 0} if more else {},
-        compiler_params=params(),
-        cost_estimate=cost(1e6, count * 200e3),
+        compiler_params=params(16),
+        cost_estimate=cost(1e6, 1e5),
         name="unpack",
-    )(spot, *pieces, *more)
+    )(spot, *pieces)
 
 
 def along_y(value, steps):
@@ -492,37 +524,31 @@
     return lax.all_to_all(value, "chan", split_axis=0, concat_axis=0, tiled=True)
 
 
-def back(spot, keep, send, scaling):
+def gather_sums(spot, keep, send):
     got = other_core(send)
     own, *rest = core_sum(spot, keep, got)
-    parts = [own] + [along_y(piece, k + 1) for k, piece in enumerate(rest)]
-    mine = factor(parts, scaling)
+    return [own] + [along_y(piece, k + 1) for k, piece in enumerate(rest)]
+
+
+def share_factors(mine):
     found = [mine] + [along_y(mine, k) for k in (1, 2, 3)]
     return found + [other_core(piece) for piece in found]
 
 
 def on_device(echoes, chirp, train_mask):
     w = jnp.asarray(doppler_matrices())
-    spot_range = lax.axis_index("range").astype(jnp.int32)
-    spot = jnp.stack([spot_range // 2, spot_range % 2])
-    scaling = 1.0 / (2 * TILE * 8)
+    mask = train_mask.T
+    here = lax.axis_index("range").astype(jnp.int32)
+    spot = jnp.stack([here >> 1, here & 1])
+    scaling = 1.0 / (2 * TILE * lax.axis_size("range"))
     flat0, rim = front0(chirp, echoes, w)
     halo = lax.ppermute(rim, "range", [(i, i - 1) for i in range(1, 8)])
     got0 = across(flat0.reshape(CHANS, WIDE, 8, TILE))
-    send_a, send_b = front1(chirp, echoes, halo, w)
-    got_a = across(send_a).reshape(CHANS, EARLY + 1, 8, TILE)
-    got_b = across(send_b).reshape(CHANS, LATE, 8, TILE)
-    sums0, spectra = gram0(train_mask, got0)
-    keep_a, out_a, spectra = gram1(
-        0, EARLY, spot, train_mask, sums0, [got_a], [(0, EARLY + 1)], spectra, "gram_a"
-    )
-    pieces_a = back(spot, keep_a, out_a, scaling)
-    keep_b, out_b, spectra = gram1(
-        EARLY, LATE, spot, train_mask, sums0, [got_a, got_b], [(EARLY, 1), (0, LATE)], spectra, "gram_b"
-    )
-    pieces_b = back(spot, keep_b, out_b, scaling)
-    factors = unpack(0, spot, pieces_a, None)
-    factors = unpack(EARLY, spot, pieces_b, factors)
+    got1 = across(front1(chirp, echoes, halo, w).reshape(CHANS, WIDE, 8, TILE))
+    sums0, spectra = gram0(mask, got0)
+    send, keep, spectra = gram1(spot, mask, got1, sums0, spectra)
+    mine = factor(gather_sums(spot, keep, send), scaling)
+    factors = unpack(spot, share_factors(mine))
     return spectra, factors
 
 

time: 182 us -> 153 us (0.84)
  waiting for transfers between devices: 51.6 us -> 75.6 us
  Pallas kernels: 64.2 us -> 44 us
  blocking collectives: 15.7 us -> 0 us
  starting transfers between devices: 36.9 us -> 25.5 us
  local copies, waits for them, and re-layouts: 11.6 us -> 5.86 us
    pallas_call x2 -> x1, Pallas kernels: 28.6 us -> 9.95 us  [factor(): pl.pallas_call(functools.partial(factor_kernel, scaling), in_specs=[VMEM]...]
    all_to_all x1 -> x0, blocking collectives: 15.7 us -> none  [across(): lax.all_to_all(value, 'chan', split_axis=0, concat_axis=0, tiled=True)]
    ppermute x12 -> x6, waiting for transfers between devices: 13.8 us -> 25.2 us  [along_y(): lax.ppermute(value, 'range', [(i, (i + 2 * steps) % 8) for i in range(8)])]
    ppermute x12 -> x6, starting transfers between devices: 19 us -> 8.51 us  [along_y(): lax.ppermute(value, 'range', [(i, (i + 2 * steps) % 8) for i in range(8)])]
    all_to_all x2, waiting for transfers between devices: 37.8 us -> 46.2 us  [across(): lax.all_to_all(value, 'chan', split_axis=0, concat_axis=0, tiled=True)]
    unnamed x23 -> x10, local copies, waits for them, and re-layouts: 11.6 us -> 5.86 us
    ppermute x10 -> x5, waiting for transfers between devices: 0.03 us -> 4.18 us  [other_core(): return lax.ppermute(value, 'range', [(i, i ^ 1) for i in range(8)])]
    pallas_call x5 -> x3, Pallas kernels: 20.3 us -> 16.7 us  [the longest x1 7.32 us: gram1(): pl.pallas_call(gram1_kernel, grid_spec=pltpu.PrefetchScalarGridSpec(num_s...]
  transfers between devices with their start and end apart: 25 -> 14, of which waited for: 7 -> 8; matrix products, arithmetic and copies ran while one was open for 0% -> 0% of each run, Pallas kernels for 27% -> 9%
where the time goes in v2:
time: 153 us; the launch traced here: 152 us
  waiting for transfers between devices  75.6 us (49%)
  Pallas kernels  44 us (29%)
  starting transfers between devices  25.5 us (17%)
  local copies, waits for them, and re-layouts  5.86 us (4%)
    all_to_all x2, waiting for transfers between devices, across(): lax.all_to_all(value, 'chan', split_axis=0, concat_axis=0, tiled=True)  46.2 us
    ppermute x6, waiting for transfers between devices, along_y(): lax.ppermute(value, 'range', [(i, (i + 2 * steps) % 8) for i in range(8)])  25.2 us
    all_to_all x2, starting transfers between devices, across(): lax.all_to_all(value, 'chan', split_axis=0, concat_axis=0, tiled=True)  15.2 us
    pallas_call x1, Pallas kernels, factor(): pl.pallas_call(functools.partial(factor_kernel, scaling), in_specs=[VMEM]...  9.95 us
    pallas_call x1, Pallas kernels, front0(): pl.pallas_call(front0_kernel, grid=(2,), in_specs=[pl.BlockSpec(chirp.sha...  8.51 us
    ppermute x6, starting transfers between devices, along_y(): lax.ppermute(value, 'range', [(i, (i + 2 * steps) % 8) for i in range(8)])  8.51 us
    pallas_call x1, Pallas kernels, front1(): pl.pallas_call(front1_kernel, grid=(2,), in_specs=[pl.BlockSpec(chirp.sha...  8.12 us
    pallas_call x1, Pallas kernels, gram1(): pl.pallas_call(gram1_kernel, grid_spec=pltpu.PrefetchScalarGridSpec(num_s...  7.32 us
  transfers between devices with their start and end apart: 14, of which 8 were waited for; matrix products, arithmetic and copies ran while one was open for 0% of the time, Pallas kernels for 9%

profile of v2, /device:TPU:0, one launch (start us, length us, event | category | flops | bytes accessed | tf_op | source)
XLA Modules:
  0.0 151.7 jit_solution(12300036537350519222)
XLA Ops:
  0.6 8.5 %front0.1 = (f32[4224,128]{1,0:T(8,128)}, f32[2,4,512,128]{3,2,1,0:T(8,128)}) custom-call(f32[2,129]{1,0:T(2,128)} %chirp_ref.3, f32[2,4,512,256]{3,2,1,0:T(8,128)} %x_ref.3, bf16[2,4,256,256]{3,2,1,0:T(8,128)(2,1)} %constant.10.clone.w_ref), custom_call_target="tpu_custom_call" | custom-call | flops 4000000000 | bytes 12000000 | tf_op jit(solution)/shard_map/front0/pallas_call | solution.py:155
  9.1 1.3 collective-permute-start
  10.4 8.0 %all-to-all-start.1 = ((f32[16,33,8,128]{3,2,1,0:T(8,128)}), f32[16,33,8,128]{3,2,1,0:T(8,128)S(1)}, u32[]{:S(2)}, u32[]{:S(2)}) async-start(f32[16,33,8,128]{3,2,1,0:T(8,128)} %bitcast.8), calls=%async_computation.1 | async-start | bytes 4325376 | tf_op jit(solution)/shard_map/all_to_all | solution.py:524
  18.4 8.1 %front1.1 = f32[4224,128]{1,0:T(8,128)} custom-call(f32[2,129]{1,0:T(2,128)} %chirp_ref.3, f32[2,4,512,256]{3,2,1,0:T(8,128)} %x_ref.3, f32[2,4,512,128]{3,2,1,0:T(8,128)} %collective-permute-done.h_ref, bf16[2,4,256,256]{3,2,1,0:T(8,128)(2,1)} %constant.10.clone.w_ref), custom_call_target="tpu_custom_call" | custom-call | flops 4000000000 | bytes 8000000 | tf_op jit(solution)/shard_map/front1/pallas_call | solution.py:179
  26.5 23.9 %all-to-all-done.1.r_ref.edge_ref = f32[16,33,8,128]{3,2,1,0:T(8,128)S(1)} async-done(((f32[16,33,8,128]{3,2,1,0:T(8,128)}), f32[16,33,8,128]{3,2,1,0:T(8,128)S(1)}, u32[]{:S(2)}, u32[]{:S(2)}) %all-to-all-start.1) | async-done | bytes 2162720 | tf_op jit(solution)/shard_map/all_to_all | solution.py:524
  50.4 1.3 copy-done
  51.7 7.2 %all-to-all-start = ((f32[16,33,8,128]{3,2,1,0:T(8,128)}), f32[16,33,8,128]{3,2,1,0:T(8,128)S(1)}, u32[]{:S(2)}, u32[]{:S(2)}) async-start(f32[16,33,8,128]{3,2,1,0:T(8,128)} %bitcast.7), calls=%async_computation | async-start | bytes 4325376 | tf_op jit(solution)/shard_map/all_to_all | solution.py:524
  59.0 1.6 %copy-done.1 = f32[16,33,8,128]{3,2,1,0:T(8,128)S(1)} copy-done((f32[16,33,8,128]{3,2,1,0:T(8,128)S(1)}, f32[16,33,8,128]{3,2,1,0:T(8,128)}, u32[]{:S(2)}) %copy-start.1) | copy-done | bytes 2162712
  60.6 6.2 %gram0.1 = (f32[32,128,128]{2,1,0:T(8,128)S(1)}, bf16[2,32,64,256]{3,2,1,0:T(8,128)(2,1)}) custom-call(s32[2,32]{1,0:T(2,128)S(1)} %bitcast.5, f32[16,33,8,128]{3,2,1,0:T(8,128)S(1)} %copy-done.1, f32[16,33,8,128]{3,2,1,0:T(8,128)S(1)} %copy-done.1), custom_call_target="tpu_custom_call" | custom-call | flops 2000000000 | bytes 6000000 | tf_op jit(solution)/shard_map/gram0/pallas_call | solution.py:256
  66.8 1.3 copy-done.2
  68.1 22.3 %all-to-all-done.r_ref.edge_ref = f32[16,33,8,128]{3,2,1,0:T(8,128)S(1)} async-done(((f32[16,33,8,128]{3,2,1,0:T(8,128)}), f32[16,33,8,128]{3,2,1,0:T(8,128)S(1)}, u32[]{:S(2)}, u32[]{:S(2)}) %all-to-all-start) | async-done | bytes 2162720 | tf_op jit(solution)/shard_map/all_to_all | solution.py:524
  90.4 1.6 %copy-done.3 = f32[32,128,128]{2,1,0:T(8,128)S(1)} copy-done((f32[32,128,128]{2,1,0:T(8,128)S(1)}, f32[32,128,128]{2,1,0:T(8,128)}, u32[]{:S(2)}) %copy-start.3) | copy-done | bytes 2097176
  92.0 7.3 %gram1.1 = (f32[16,128,128]{2,1,0:T(8,128)S(1)}, f32[16,128,128]{2,1,0:T(8,128)S(1)}, bf16[2,32,64,256]{3,2,1,0:T(8,128)(2,1)}) custom-call(s32[2]{0:T(128)S(1)} %pad_add_fusion.spot_ref, s32[2,32]{1,0:T(2,128)S(1)} %bitcast.6, f32[16,33,8,128]{3,2,1,0:T(8,128)S(1)} %all-to-all-done.r_ref.edge_ref, ...), custom_call_target="tpu_custom_call", output_to_operand_aliasing={{2}: (5, {})} | custom-call | flops 2000000000 | bytes 6000000 | tf_op jit(solution)/shard_map/gram1/pallas_call | solution.py:306
  99.3 2.7 %collective-permute-done.1.got_ref = f32[16,128,128]{2,1,0:T(8,128)S(1)} collective-permute-done((f32[16,128,128]{2,1,0:T(8,128)S(1)}, f32[16,128,128]{2,1,0:T(8,128)S(1)}, u32[]{:S(2)}, u32[]{:S(2)}) %collective-permute-start.1) | collective-permute-done | bytes 1048608 | tf_op jit(solution)/shard_map/ppermute | solution.py:520
  102.7 5.3 %collective-permute-start.3 = (f32[4,128,128]{2,1,0:T(8,128)S(1)}, f32[4,128,128]{2,1,0:T(8,128)S(1)}, u32[]{:S(2)}, u32[]{:S(2)}) collective-permute-start(f32[4,128,128]{2,1,0:T(8,128)S(1)} %get-tuple-element.22), channel_id=1, source_target_pairs={{0,64},{16,80},{32,96},{48,112},{64,0},{80,16},{96,32},{112,48},{1... | collective-permute-start | bytes 786440 | tf_op jit(solution)/shard_map/ppermute | solution.py:516
  108.0 5.1 %collective-permute-done.2.refs_1_ = f32[4,128,128]{2,1,0:T(8,128)S(1)} collective-permute-done((f32[4,128,128]{2,1,0:T(8,128)S(1)}, f32[4,128,128]{2,1,0:T(8,128)S(1)}, u32[]{:S(2)}, u32[]{:S(2)}) %collective-permute-start.2) | collective-permute-done | bytes 262176 | tf_op jit(solution)/shard_map/ppermute | solution.py:516
  113.2 6.8 %collective-permute-done.3.refs_2_ = f32[4,128,128]{2,1,0:T(8,128)S(1)} collective-permute-done((f32[4,128,128]{2,1,0:T(8,128)S(1)}, f32[4,128,128]{2,1,0:T(8,128)S(1)}, u32[]{:S(2)}, u32[]{:S(2)}) %collective-permute-start.3) | collective-permute-done | bytes 262176 | tf_op jit(solution)/shard_map/ppermute | solution.py:516
  119.9 10.0 %factor.1.refs_0_ = f32[4,128,128]{2,1,0:T(8,128)S(1)} custom-call(f32[4,128,128]{2,1,0:T(8,128)S(1)} %get-tuple-element.20.refs_0_, f32[4,128,128]{2,1,0:T(8,128)S(1)} %collective-permute-done.2.refs_1_, f32[4,128,128]{2,1,0:T(8,128)S(1)} %collective-permute-done.3.refs_2_, f32[4,128,128]{2,1,0:T(8,128)S(1)} %collective-permute-done.4.refs_3_), custom_call_target="tpu_custom_call" | custom-call | flops 1000000 | bytes 100000 | tf_op jit(solution)/shard_map/factor/pallas_call | solution.py:470
  129.9 2.2 %collective-permute-start.7 = (f32[4,128,128]{2,1,0:T(8,128)S(1)}, f32[4,128,128]{2,1,0:T(8,128)S(1)}, u32[]{:S(2)}, u32[]{:S(2)}) collective-permute-start(f32[4,128,128]{2,1,0:T(8,128)S(1)} %factor.1.refs_0_), channel_id=1, source_target_pairs={{0,96},{16,112},{32,0},{48,16},{64,32},{80,48},{96,64},{112,80},{1... | collective-permute-start | bytes 786440 | tf_op jit(solution)/shard_map/ppermute | solution.py:516
  132.1 0.9 collective-permute-start.5
  133.1 10.4 %collective-permute-done.7.refs_3_ = f32[4,128,128]{2,1,0:T(8,128)S(1)} collective-permute-done((f32[4,128,128]{2,1,0:T(8,128)S(1)}, f32[4,128,128]{2,1,0:T(8,128)S(1)}, u32[]{:S(2)}, u32[]{:S(2)}) %collective-permute-start.7) | collective-permute-done | bytes 262176 | tf_op jit(solution)/shard_map/ppermute | solution.py:516
  144.0 2.9 %collective-permute-done.5.refs_1_ = f32[4,128,128]{2,1,0:T(8,128)S(1)} collective-permute-done((f32[4,128,128]{2,1,0:T(8,128)S(1)}, f32[4,128,128]{2,1,0:T(8,128)S(1)}, u32[]{:S(2)}, u32[]{:S(2)}) %collective-permute-start.5) | collective-permute-done | bytes 262176 | tf_op jit(solution)/shard_map/ppermute | solution.py:516
  146.9 1.5 collective-permute-done.9.refs_5_
  148.4 3.3 %unpack.1 = f32[32,2,128,128]{3,2,1,0:T(8,128)} custom-call(s32[2]{0:T(128)S(1)} %pad_add_fusion.spot_ref, f32[4,128,128]{2,1,0:T(8,128)S(1)} %factor.1.refs_0_, f32[4,128,128]{2,1,0:T(8,128)S(1)} %collective-permute-done.5.refs_1_, f32[4,128,128]{2,1,0:T(8,128)S(1)} %collective-permute-done.6.refs_2_, f32[4,128,128]{2,1,0:T(8,128)S(1)} %collective-permute-done.7.refs_3_, ...), custom_call_target="tpu_custom_call" | custom-call | flops 1000000 | bytes 100000 | tf_op jit(solution)/shard_map/unpack/pallas_call | solution.py:504
  (22 shorter events, 1.4 us)
Async XLA Ops:
  9.1 9.3 %collective-permute-start = (f32[2,4,512,128]{3,2,1,0:T(8,128)}, f32[2,4,512,128]{3,2,1,0:T(8,128)}, u32[]{:S(2)}, u32[]{:S(2)}) collective-permute-start(f32[2,4,512,128]{3,2,1,0:T(8,128)} %get-tuple-element.13), channel_id=1, source_target_pairs={{16,0},{32,16},{48,32},{64,48},{80,64},{96,80},{112,96},{17,1},{33... | collective-permute-start | bytes 6291464 | tf_op jit(solution)/shard_map/ppermute | solution.py:545
  10.4 40.0 %all-to-all-start.1 = ((f32[16,33,8,128]{3,2,1,0:T(8,128)}), f32[16,33,8,128]{3,2,1,0:T(8,128)S(1)}, u32[]{:S(2)}, u32[]{:S(2)}) async-start(f32[16,33,8,128]{3,2,1,0:T(8,128)} %bitcast.8), calls=%async_computation.1 | async-start | bytes 4325376 | tf_op jit(solution)/shard_map/all_to_all | solution.py:524
  50.4 1.3 copy-start
  51.7 7.3 %copy-start.4 = (s32[32,2]{0,1:T(2,128)S(1)}, s32[32,2]{0,1:T(2,128)}, u32[]{:S(2)}) copy-start(s32[32,2]{0,1:T(2,128)} %param.6) | copy-start | bytes 772
  51.7 38.7 %all-to-all-start = ((f32[16,33,8,128]{3,2,1,0:T(8,128)}), f32[16,33,8,128]{3,2,1,0:T(8,128)S(1)}, u32[]{:S(2)}, u32[]{:S(2)}) async-start(f32[16,33,8,128]{3,2,1,0:T(8,128)} %bitcast.7), calls=%async_computation | async-start | bytes 4325376 | tf_op jit(solution)/shard_map/all_to_all | solution.py:524
  59.0 1.6 %copy-start.1 = (f32[16,33,8,128]{3,2,1,0:T(8,128)S(1)}, f32[16,33,8,128]{3,2,1,0:T(8,128)}, u32[]{:S(2)}) copy-start(f32[16,33,8,128]{3,2,1,0:T(8,128)} %copy-done) | copy-start | bytes 6488068
  66.8 1.3 copy-start.2
  90.4 1.6 %copy-start.3 = (f32[32,128,128]{2,1,0:T(8,128)S(1)}, f32[32,128,128]{2,1,0:T(8,128)}, u32[]{:S(2)}) copy-start(f32[32,128,128]{2,1,0:T(8,128)} %copy-done.2) | copy-start | bytes 6291460
  99.3 2.7 %collective-permute-start.1 = (f32[16,128,128]{2,1,0:T(8,128)S(1)}, f32[16,128,128]{2,1,0:T(8,128)S(1)}, u32[]{:S(2)}, u32[]{:S(2)}) collective-permute-start(f32[16,128,128]{2,1,0:T(8,128)S(1)} %get-tuple-element.19), channel_id=1, source_target_pairs={{0,16},{16,0},{32,48},{48,32},{64,80},{80,64},{96,112},{112,96},{1... | collective-permute-start | bytes 3145736 | tf_op jit(solution)/shard_map/ppermute | solution.py:520
  102.7 10.5 %collective-permute-start.2 = (f32[4,128,128]{2,1,0:T(8,128)S(1)}, f32[4,128,128]{2,1,0:T(8,128)S(1)}, u32[]{:S(2)}, u32[]{:S(2)}) collective-permute-start(f32[4,128,128]{2,1,0:T(8,128)S(1)} %get-tuple-element.21), channel_id=1, source_target_pairs={{0,32},{16,48},{32,64},{48,80},{64,96},{80,112},{96,0},{112,16},{1... | collective-permute-start | bytes 786440 | tf_op jit(solution)/shard_map/ppermute | solution.py:516
  102.7 17.2 %collective-permute-start.3 = (f32[4,128,128]{2,1,0:T(8,128)S(1)}, f32[4,128,128]{2,1,0:T(8,128)S(1)}, u32[]{:S(2)}, u32[]{:S(2)}) collective-permute-start(f32[4,128,128]{2,1,0:T(8,128)S(1)} %get-tuple-element.22), channel_id=1, source_target_pairs={{0,64},{16,80},{32,96},{48,112},{64,0},{80,16},{96,32},{112,48},{1... | collective-permute-start | bytes 786440 | tf_op jit(solution)/shard_map/ppermute | solution.py:516
  108.0 11.9 %collective-permute-start.4 = (f32[4,128,128]{2,1,0:T(8,128)S(1)}, f32[4,128,128]{2,1,0:T(8,128)S(1)}, u32[]{:S(2)}, u32[]{:S(2)}) collective-permute-start(f32[4,128,128]{2,1,0:T(8,128)S(1)} %get-tuple-element.23), channel_id=1, source_target_pairs={{0,96},{16,112},{32,0},{48,16},{64,32},{80,48},{96,64},{112,80},{1... | collective-permute-start | bytes 786440 | tf_op jit(solution)/shard_map/ppermute | solution.py:516
  129.9 13.6 %collective-permute-start.7 = (f32[4,128,128]{2,1,0:T(8,128)S(1)}, f32[4,128,128]{2,1,0:T(8,128)S(1)}, u32[]{:S(2)}, u32[]{:S(2)}) collective-permute-start(f32[4,128,128]{2,1,0:T(8,128)S(1)} %factor.1.refs_0_), channel_id=1, source_target_pairs={{0,96},{16,112},{32,0},{48,16},{64,32},{80,48},{96,64},{112,80},{1... | collective-permute-start | bytes 786440 | tf_op jit(solution)/shard_map/ppermute | solution.py:516
  132.1 11.4 %collective-permute-start.6 = (f32[4,128,128]{2,1,0:T(8,128)S(1)}, f32[4,128,128]{2,1,0:T(8,128)S(1)}, u32[]{:S(2)}, u32[]{:S(2)}) collective-permute-start(f32[4,128,128]{2,1,0:T(8,128)S(1)} %factor.1.refs_0_), channel_id=1, source_target_pairs={{0,64},{16,80},{32,96},{48,112},{64,0},{80,16},{96,32},{112,48},{1... | collective-permute-start | bytes 786440 | tf_op jit(solution)/shard_map/ppermute | solution.py:516
  132.1 14.8 %collective-permute-start.5 = (f32[4,128,128]{2,1,0:T(8,128)S(1)}, f32[4,128,128]{2,1,0:T(8,128)S(1)}, u32[]{:S(2)}, u32[]{:S(2)}) collective-permute-start(f32[4,128,128]{2,1,0:T(8,128)S(1)} %factor.1.refs_0_), channel_id=1, source_target_pairs={{0,32},{16,48},{32,64},{48,80},{64,96},{80,112},{96,0},{112,16},{1... | collective-permute-start | bytes 786440 | tf_op jit(solution)/shard_map/ppermute | solution.py:516
  133.1 13.8 %collective-permute-start.8 = (f32[4,128,128]{2,1,0:T(8,128)S(1)}, f32[4,128,128]{2,1,0:T(8,128)S(1)}, u32[]{:S(2)}, u32[]{:S(2)}) collective-permute-start(f32[4,128,128]{2,1,0:T(8,128)S(1)} %factor.1.refs_0_), channel_id=1, source_target_pairs={{0,16},{16,0},{32,48},{48,32},{64,80},{80,64},{96,112},{112,96},{1... | collective-permute-start | bytes 786440 | tf_op jit(solution)/shard_map/ppermute | solution.py:520
  143.5 3.4 %collective-permute-start.11 = (f32[4,128,128]{2,1,0:T(8,128)S(1)}, f32[4,128,128]{2,1,0:T(8,128)S(1)}, u32[]{:S(2)}, u32[]{:S(2)}) collective-permute-start(f32[4,128,128]{2,1,0:T(8,128)S(1)} %collective-permute-done.7.refs_3_), channel_id=1, source_target_pairs={{0,16},{16,0},{32,48},{48,32},{64,80},{80,64},{96,112},{112,96},{1... | collective-permute-start | bytes 786440 | tf_op jit(solution)/shard_map/ppermute | solution.py:520
  143.5 3.4 %collective-permute-start.10 = (f32[4,128,128]{2,1,0:T(8,128)S(1)}, f32[4,128,128]{2,1,0:T(8,128)S(1)}, u32[]{:S(2)}, u32[]{:S(2)}) collective-permute-start(f32[4,128,128]{2,1,0:T(8,128)S(1)} %collective-permute-done.6.refs_2_), channel_id=1, source_target_pairs={{0,16},{16,0},{32,48},{48,32},{64,80},{80,64},{96,112},{112,96},{1... | collective-permute-start | bytes 786440 | tf_op jit(solution)/shard_map/ppermute | solution.py:520
  146.9 1.5 %collective-permute-start.9 = (f32[4,128,128]{2,1,0:T(8,128)S(1)}, f32[4,128,128]{2,1,0:T(8,128)S(1)}, u32[]{:S(2)}, u32[]{:S(2)}) collective-permute-start(f32[4,128,128]{2,1,0:T(8,128)S(1)} %collective-permute-done.5.refs_1_), channel_id=1, source_target_pairs={{0,16},{16,0},{32,48},{48,32},{64,80},{80,64},{96,112},{112,96},{1... | collective-permute-start | bytes 786440 | tf_op jit(solution)/shard_map/ppermute | solution.py:520

commit v3 on v2

--- a/solution.py
+++ b/solution.py
@@ -276,38 +276,27 @@
     )(mask, received, received)
 
 
-def gram1_kernel(spot_ref, mask_ref, r_ref, edge_ref, sums_ref, _, send_ref, keep_ref, spectra_ref, high_ref, low_ref):
-    steps = BINS // GROUP
-    step = pl.program_id(0)
-    first = lax.rem(step + (1 - spot_ref[1]) * (steps // 2), steps) * GROUP
+def gram1_kernel(other, spot_ref, mask_ref, r_ref, edge_ref, sums_ref, _, out_ref, spectra_ref, high_ref, low_ref):
+    core = spot_ref[1]
+    half = BINS // GROUP // 2
+    first = ((1 - core if other else core) * half + pl.program_id(0)) * GROUP
     plant_all(r_ref, edge_ref, spectra_ref, high_ref, low_ref)
-
-    def fill(out_ref):
-        for b in range(GROUP):
-            weight = mask_ref[1, first + b].astype(F32)
-            out_ref[b] = sums_ref[b] + bin_gram(b, high_ref, low_ref) * weight
-
-    @pl.when(step < steps // 2)
-    def _():
-        fill(send_ref)
-
-    @pl.when(step >= steps // 2)
-    def _():
-        fill(keep_ref)
-
-
-def gram1(spot, mask, received, sums, spectra):
-    steps = BINS // GROUP
-    half = steps // 2
+    for b in range(GROUP):
+        weight = mask_ref[1, first + b].astype(F32)
+        out_ref[b] = sums_ref[b] + bin_gram(b, high_ref, low_ref) * weight
+
+
+def gram1(other, spot, mask, received, sums, spectra, name):
+    half = BINS // GROUP // 2
 
     def at(i, spot):
-        return lax.rem(i + (1 - spot[1]) * half, steps)
-
-    return pl.pallas_call(
-        gram1_kernel,
+        return (1 - spot[1] if other else spot[1]) * half + i
+
+    return pl.pallas_call(
+        functools.partial(gram1_kernel, other),
         grid_spec=pltpu.PrefetchScalarGridSpec(
             num_scalar_prefetch=1,
-            grid=(steps,),
+            grid=(half,),
             in_specs=[
                 SMEM,
                 pl.BlockSpec((CHANS, GROUP, 8, TILE), lambda i, spot: (0, at(i, spot), 0, 0)),
@@ -316,18 +305,19 @@
                 ANY,
             ],
             out_specs=[
-                pl.BlockSpec((GROUP, 128, 128), lambda i, spot: (jnp.minimum(i, half - 1), 0, 0)),
-                pl.BlockSpec((GROUP, 128, 128), lambda i, spot: (jnp.maximum(i - half, 0), 0, 0)),
+                pl.BlockSpec((GROUP, 128, 128), lambda i, spot: (i, 0, 0)),
                 pl.BlockSpec((2, GROUP, 64, TILE), lambda i, spot: (0, at(i, spot), 0, 1)),
             ],
             scratch_shapes=gram_scratch(GROUP),
         ),
-        out_shape=[jax.ShapeDtypeStruct((BINS // 2, 128, 128), F32)] * 2
-        + [jax.ShapeDtypeStruct(spectra.shape, spectra.dtype)],
-        input_output_aliases={5: 2},
+        out_shape=[
+            jax.ShapeDtypeStruct((BINS // 2, 128, 128), F32),
+            jax.ShapeDtypeStruct(spectra.shape, spectra.dtype),
+        ],
+        input_output_aliases={5: 1},
         compiler_params=params(20),
         cost_estimate=cost(2e9, 6e6),
-        name="gram1",
+        name=name,
     )(spot, mask, received, received, sums, spectra)
 
 
@@ -480,23 +470,27 @@
 
 
 def unpack_kernel(share, spot_ref, *refs):
-    pieces, out_ref = refs[:8], refs[-1]
+    pieces, out_ref, held_ref, sems = refs[:8], refs[8], refs[9], refs[10]
     row = lax.broadcasted_iota(jnp.int32, (128, 128), 0)
     column = lax.broadcasted_iota(jnp.int32, (128, 128), 1)
     y, core = spot_ref[0], spot_ref[1]
+    copies = []
     for k in range(8):
         steps, other = k % 4, k // 4
         owner = lax.rem(y + 4 - steps, 4)
         whose = core + other - 2 * core * other
         base = (whose * 4 + owner) * share
-
-        def one(i, carry, piece=pieces[k], base=base):
-            packed = piece[i]
-            out_ref[base + i, 0] = jnp.where(row <= column, packed, 0.0)
-            out_ref[base + i, 1] = jnp.where(row < column, packed.T, 0.0)
-            return carry
-
-        lax.fori_loop(0, share, one, 0, unroll=True)
+        for i in range(share):
+            packed = pieces[k][i]
+            held_ref[k * share + i, 0] = jnp.where(row <= column, packed, 0.0)
+            held_ref[k * share + i, 1] = jnp.where(row < column, packed.T, 0.0)
+        copy = pltpu.make_async_copy(
+            held_ref.at[pl.ds(k * share, share)], out_ref.at[pl.ds(base, share)], sems.at[k]
+        )
+        copy.start()
+        copies.append(copy)
+    for copy in copies:
+        copy.wait()
 
 
 def unpack(spot, pieces):
@@ -504,8 +498,12 @@
     return pl.pallas_call(
         functools.partial(unpack_kernel, share),
         in_specs=[SMEM] + [VMEM] * 8,
-        out_specs=VMEM,
+        out_specs=ANY,
         out_shape=jax.ShapeDtypeStruct((BINS, 2, 128, 128), F32),
+        scratch_shapes=[
+            pltpu.VMEM((8 * share, 2, 128, 128), F32),
+            pltpu.SemaphoreType.DMA((8,)),
+        ],
         compiler_params=params(16),
         cost_estimate=cost(1e6, 1e5),
         name="unpack",
@@ -546,7 +544,8 @@
     got0 = across(flat0.reshape(CHANS, WIDE, 8, TILE))
     got1 = across(front1(chirp, echoes, halo, w).reshape(CHANS, WIDE, 8, TILE))
     sums0, spectra = gram0(mask, got0)
-    send, keep, spectra = gram1(spot, mask, got1, sums0, spectra)
+    send, spectra = gram1(True, spot, mask, got1, sums0, spectra, "gram1_send")
+    keep, spectra = gram1(False, spot, mask, got1, sums0, spectra, "gram1_keep")
     mine = factor(gather_sums(spot, keep, send), scaling)
     factors = unpack(spot, share_factors(mine))
     return spectra, factors

time: 153 us -> 152 us (level)
  waiting for transfers between devices: 75.6 us -> 73.3 us
    ppermute x5, waiting for transfers between devices: 4.18 us -> 1.52 us  [other_core(): return lax.ppermute(value, 'range', [(i, i ^ 1) for i in range(8)])]
    pallas_call x1 -> x2, Pallas kernels: 7.32 us -> 8.51 us  [gram1(): pl.pallas_call(functools.partial(gram1_kernel, other), grid_spec=pltpu.Pr...]
  transfers between devices with their start and end apart: 14 -> 14, of which waited for: 8 -> 7; matrix products, arithmetic and copies ran while one was open for 0% -> 0% of each run, Pallas kernels for 9% -> 12%
where the time goes in v3:
time: 152 us; the launch traced here: 150 us
  waiting for transfers between devices  73.3 us (48%)
  Pallas kernels  44.6 us (29%)
  starting transfers between devices  25.5 us (17%)
  local copies, waits for them, and re-layouts  5.86 us (4%)
    all_to_all x2, waiting for transfers between devices, across(): lax.all_to_all(value, 'chan', split_axis=0, concat_axis=0, tiled=True)  46.2 us
    ppermute x6, waiting for transfers between devices, along_y(): lax.ppermute(value, 'range', [(i, (i + 2 * steps) % 8) for i in range(8)])  25.6 us
    all_to_all x2, starting transfers between devices, across(): lax.all_to_all(value, 'chan', split_axis=0, concat_axis=0, tiled=True)  15.2 us
    pallas_call x1, Pallas kernels, factor(): pl.pallas_call(functools.partial(factor_kernel, scaling), in_specs=[VMEM]...  9.95 us
    ppermute x6, starting transfers between devices, along_y(): lax.ppermute(value, 'range', [(i, (i + 2 * steps) % 8) for i in range(8)])  8.54 us
    pallas_call x1, Pallas kernels, front0(): pl.pallas_call(front0_kernel, grid=(2,), in_specs=[pl.BlockSpec(chirp.sha...  8.51 us
    pallas_call x2, Pallas kernels, gram1(): pl.pallas_call(functools.partial(gram1_kernel, other), grid_spec=pltpu.Pr...  8.51 us
    pallas_call x1, Pallas kernels, front1(): pl.pallas_call(front1_kernel, grid=(2,), in_specs=[pl.BlockSpec(chirp.sha...  8.12 us
  transfers between devices with their start and end apart: 14, of which 7 were waited for; matrix products, arithmetic and copies ran while one was open for 0% of the time, Pallas kernels for 12%

profile of v3, /device:TPU:0, one launch (start us, length us, event | category | flops | bytes accessed | tf_op | source)
XLA Modules:
  0.0 150.3 jit_solution(10163794878257518444)
XLA Ops:
  0.6 8.5 %front0.1 = (f32[4224,128]{1,0:T(8,128)}, f32[2,4,512,128]{3,2,1,0:T(8,128)}) custom-call(f32[2,129]{1,0:T(2,128)} %chirp_ref.3, f32[2,4,512,256]{3,2,1,0:T(8,128)} %x_ref.3, bf16[2,4,256,256]{3,2,1,0:T(8,128)(2,1)} %constant.10.clone.w_ref), custom_call_target="tpu_custom_call" | custom-call | flops 4000000000 | bytes 12000000 | tf_op jit(solution)/shard_map/front0/pallas_call | solution.py:155
  9.1 1.3 collective-permute-start
  10.4 8.0 %all-to-all-start.1 = ((f32[16,33,8,128]{3,2,1,0:T(8,128)}), f32[16,33,8,128]{3,2,1,0:T(8,128)S(1)}, u32[]{:S(2)}, u32[]{:S(2)}) async-start(f32[16,33,8,128]{3,2,1,0:T(8,128)} %bitcast.9), calls=%async_computation.1 | async-start | bytes 4325376 | tf_op jit(solution)/shard_map/all_to_all | solution.py:522
  18.4 8.1 %front1.1 = f32[4224,128]{1,0:T(8,128)} custom-call(f32[2,129]{1,0:T(2,128)} %chirp_ref.3, f32[2,4,512,256]{3,2,1,0:T(8,128)} %x_ref.3, f32[2,4,512,128]{3,2,1,0:T(8,128)} %collective-permute-done.h_ref, bf16[2,4,256,256]{3,2,1,0:T(8,128)(2,1)} %constant.10.clone.w_ref), custom_call_target="tpu_custom_call" | custom-call | flops 4000000000 | bytes 8000000 | tf_op jit(solution)/shard_map/front1/pallas_call | solution.py:179
  26.5 23.9 %all-to-all-done.1.r_ref.edge_ref = f32[16,33,8,128]{3,2,1,0:T(8,128)S(1)} async-done(((f32[16,33,8,128]{3,2,1,0:T(8,128)}), f32[16,33,8,128]{3,2,1,0:T(8,128)S(1)}, u32[]{:S(2)}, u32[]{:S(2)}) %all-to-all-start.1) | async-done | bytes 2162720 | tf_op jit(solution)/shard_map/all_to_all | solution.py:522
  50.4 1.3 copy-done.2
  51.7 7.2 %all-to-all-start = ((f32[16,33,8,128]{3,2,1,0:T(8,128)}), f32[16,33,8,128]{3,2,1,0:T(8,128)S(1)}, u32[]{:S(2)}, u32[]{:S(2)}) async-start(f32[16,33,8,128]{3,2,1,0:T(8,128)} %bitcast.8), calls=%async_computation | async-start | bytes 4325376 | tf_op jit(solution)/shard_map/all_to_all | solution.py:522
  59.0 1.6 %copy-done.3 = f32[16,33,8,128]{3,2,1,0:T(8,128)S(1)} copy-done((f32[16,33,8,128]{3,2,1,0:T(8,128)S(1)}, f32[16,33,8,128]{3,2,1,0:T(8,128)}, u32[]{:S(2)}) %copy-start.3) | copy-done | bytes 2162712
  60.6 6.2 %gram0.1 = (f32[32,128,128]{2,1,0:T(8,128)S(1)}, bf16[2,32,64,256]{3,2,1,0:T(8,128)(2,1)}) custom-call(s32[2,32]{1,0:T(2,128)S(1)} %bitcast.5, f32[16,33,8,128]{3,2,1,0:T(8,128)S(1)} %copy-done.3, f32[16,33,8,128]{3,2,1,0:T(8,128)S(1)} %copy-done.3), custom_call_target="tpu_custom_call" | custom-call | flops 2000000000 | bytes 6000000 | tf_op jit(solution)/shard_map/gram0/pallas_call | solution.py:256
  66.8 1.3 copy-done
  68.1 22.3 %all-to-all-done.r_ref.edge_ref = f32[16,33,8,128]{3,2,1,0:T(8,128)S(1)} async-done(((f32[16,33,8,128]{3,2,1,0:T(8,128)}), f32[16,33,8,128]{3,2,1,0:T(8,128)S(1)}, u32[]{:S(2)}, u32[]{:S(2)}) %all-to-all-start) | async-done | bytes 2162720 | tf_op jit(solution)/shard_map/all_to_all | solution.py:522
  90.4 1.6 %copy-done.1 = f32[32,128,128]{2,1,0:T(8,128)S(1)} copy-done((f32[32,128,128]{2,1,0:T(8,128)S(1)}, f32[32,128,128]{2,1,0:T(8,128)}, u32[]{:S(2)}) %copy-start.1) | copy-done | bytes 2097176
  92.0 4.2 %gram1_send.1 = (f32[16,128,128]{2,1,0:T(8,128)S(1)}, bf16[2,32,64,256]{3,2,1,0:T(8,128)(2,1)}) custom-call(s32[2]{0:T(128)S(1)} %pad_add_fusion.spot_ref, s32[2,32]{1,0:T(2,128)S(1)} %bitcast.6, f32[16,33,8,128]{3,2,1,0:T(8,128)S(1)} %all-to-all-done.r_ref.edge_ref, ...), custom_call_target="tpu_custom_call", output_to_operand_aliasing={{1}: (5, {})} | custom-call | flops 2000000000 | bytes 6000000 | tf_op jit(solution)/shard_map/gram1_send/pallas_call | solution.py:295
  96.3 4.3 %gram1_keep.1 = (f32[16,128,128]{2,1,0:T(8,128)S(1)}, bf16[2,32,64,256]{3,2,1,0:T(8,128)(2,1)}) custom-call(s32[2]{0:T(128)S(1)} %pad_add_fusion.spot_ref, s32[2,32]{1,0:T(2,128)S(1)} %bitcast.7, f32[16,33,8,128]{3,2,1,0:T(8,128)S(1)} %all-to-all-done.r_ref.edge_ref, ...), custom_call_target="tpu_custom_call", output_to_operand_aliasing={{1}: (5, {})} | custom-call | flops 2000000000 | bytes 6000000 | tf_op jit(solution)/shard_map/gram1_keep/pallas_call | solution.py:295
  101.3 5.3 %collective-permute-start.3 = (f32[4,128,128]{2,1,0:T(8,128)S(1)}, f32[4,128,128]{2,1,0:T(8,128)S(1)}, u32[]{:S(2)}, u32[]{:S(2)}) collective-permute-start(f32[4,128,128]{2,1,0:T(8,128)S(1)} %get-tuple-element.24), channel_id=1, source_target_pairs={{0,64},{16,80},{32,96},{48,112},{64,0},{80,16},{96,32},{112,48},{1... | collective-permute-start | bytes 786440 | tf_op jit(solution)/shard_map/ppermute | solution.py:514
  106.6 5.5 %collective-permute-done.2.refs_1_ = f32[4,128,128]{2,1,0:T(8,128)S(1)} collective-permute-done((f32[4,128,128]{2,1,0:T(8,128)S(1)}, f32[4,128,128]{2,1,0:T(8,128)S(1)}, u32[]{:S(2)}, u32[]{:S(2)}) %collective-permute-start.2) | collective-permute-done | bytes 262176 | tf_op jit(solution)/shard_map/ppermute | solution.py:514
  112.1 6.8 %collective-permute-done.3.refs_2_ = f32[4,128,128]{2,1,0:T(8,128)S(1)} collective-permute-done((f32[4,128,128]{2,1,0:T(8,128)S(1)}, f32[4,128,128]{2,1,0:T(8,128)S(1)}, u32[]{:S(2)}, u32[]{:S(2)}) %collective-permute-start.3) | collective-permute-done | bytes 262176 | tf_op jit(solution)/shard_map/ppermute | solution.py:514
  118.9 10.0 %factor.1.refs_0_ = f32[4,128,128]{2,1,0:T(8,128)S(1)} custom-call(f32[4,128,128]{2,1,0:T(8,128)S(1)} %get-tuple-element.22.refs_0_, f32[4,128,128]{2,1,0:T(8,128)S(1)} %collective-permute-done.2.refs_1_, f32[4,128,128]{2,1,0:T(8,128)S(1)} %collective-permute-done.3.refs_2_, f32[4,128,128]{2,1,0:T(8,128)S(1)} %collective-permute-done.4.refs_3_), custom_call_target="tpu_custom_call" | custom-call | flops 1000000 | bytes 100000 | tf_op jit(solution)/shard_map/factor/pallas_call | solution.py:460
  128.8 2.2 %collective-permute-start.7 = (f32[4,128,128]{2,1,0:T(8,128)S(1)}, f32[4,128,128]{2,1,0:T(8,128)S(1)}, u32[]{:S(2)}, u32[]{:S(2)}) collective-permute-start(f32[4,128,128]{2,1,0:T(8,128)S(1)} %factor.1.refs_0_), channel_id=1, source_target_pairs={{0,96},{16,112},{32,0},{48,16},{64,32},{80,48},{96,64},{112,80},{1... | collective-permute-start | bytes 786440 | tf_op jit(solution)/shard_map/ppermute | solution.py:514
  131.1 0.9 collective-permute-start.5
  132.0 10.5 %collective-permute-done.7.refs_3_ = f32[4,128,128]{2,1,0:T(8,128)S(1)} collective-permute-done((f32[4,128,128]{2,1,0:T(8,128)S(1)}, f32[4,128,128]{2,1,0:T(8,128)S(1)}, u32[]{:S(2)}, u32[]{:S(2)}) %collective-permute-start.7) | collective-permute-done | bytes 262176 | tf_op jit(solution)/shard_map/ppermute | solution.py:514
  143.0 2.9 %collective-permute-done.5.refs_1_ = f32[4,128,128]{2,1,0:T(8,128)S(1)} collective-permute-done((f32[4,128,128]{2,1,0:T(8,128)S(1)}, f32[4,128,128]{2,1,0:T(8,128)S(1)}, u32[]{:S(2)}, u32[]{:S(2)}) %collective-permute-start.5) | collective-permute-done | bytes 262176 | tf_op jit(solution)/shard_map/ppermute | solution.py:514
  145.9 1.5 %collective-permute-done.9.refs_5_ = f32[4,128,128]{2,1,0:T(8,128)S(1)} collective-permute-done((f32[4,128,128]{2,1,0:T(8,128)S(1)}, f32[4,128,128]{2,1,0:T(8,128)S(1)}, u32[]{:S(2)}, u32[]{:S(2)}) %collective-permute-start.9) | collective-permute-done | bytes 262176 | tf_op jit(solution)/shard_map/ppermute | solution.py:518
  147.4 2.7 %unpack.1 = f32[32,2,128,128]{3,2,1,0:T(8,128)} custom-call(s32[2]{0:T(128)S(1)} %pad_add_fusion.spot_ref, f32[4,128,128]{2,1,0:T(8,128)S(1)} %factor.1.refs_0_, f32[4,128,128]{2,1,0:T(8,128)S(1)} %collective-permute-done.5.refs_1_, f32[4,128,128]{2,1,0:T(8,128)S(1)} %collective-permute-done.6.refs_2_, f32[4,128,128]{2,1,0:T(8,128)S(1)} %collective-permute-done.7.refs_3_, ...), custom_call_target="tpu_custom_call" | custom-call | flops 1000000 | bytes 100000 | tf_op jit(solution)/shard_map/unpack/pallas_call | solution.py:498
  (23 shorter events, 1.4 us)
Async XLA Ops:
  9.1 9.3 %collective-permute-start = (f32[2,4,512,128]{3,2,1,0:T(8,128)}, f32[2,4,512,128]{3,2,1,0:T(8,128)}, u32[]{:S(2)}, u32[]{:S(2)}) collective-permute-start(f32[2,4,512,128]{3,2,1,0:T(8,128)} %get-tuple-element.14), channel_id=1, source_target_pairs={{16,0},{32,16},{48,32},{64,48},{80,64},{96,80},{112,96},{17,1},{33... | collective-permute-start | bytes 6291464 | tf_op jit(solution)/shard_map/ppermute | solution.py:543
  10.4 40.0 %all-to-all-start.1 = ((f32[16,33,8,128]{3,2,1,0:T(8,128)}), f32[16,33,8,128]{3,2,1,0:T(8,128)S(1)}, u32[]{:S(2)}, u32[]{:S(2)}) async-start(f32[16,33,8,128]{3,2,1,0:T(8,128)} %bitcast.9), calls=%async_computation.1 | async-start | bytes 4325376 | tf_op jit(solution)/shard_map/all_to_all | solution.py:522
  50.4 1.3 copy-start.2
  51.7 7.3 %copy-start.4 = (s32[32,2]{0,1:T(2,128)S(1)}, s32[32,2]{0,1:T(2,128)}, u32[]{:S(2)}) copy-start(s32[32,2]{0,1:T(2,128)} %param.6) | copy-start | bytes 772
  51.7 38.7 %all-to-all-start = ((f32[16,33,8,128]{3,2,1,0:T(8,128)}), f32[16,33,8,128]{3,2,1,0:T(8,128)S(1)}, u32[]{:S(2)}, u32[]{:S(2)}) async-start(f32[16,33,8,128]{3,2,1,0:T(8,128)} %bitcast.8), calls=%async_computation | async-start | bytes 4325376 | tf_op jit(solution)/shard_map/all_to_all | solution.py:522
  59.0 1.6 %copy-start.3 = (f32[16,33,8,128]{3,2,1,0:T(8,128)S(1)}, f32[16,33,8,128]{3,2,1,0:T(8,128)}, u32[]{:S(2)}) copy-start(f32[16,33,8,128]{3,2,1,0:T(8,128)} %copy-done.2) | copy-start | bytes 6488068
  66.8 1.3 copy-start
  90.4 1.6 %copy-start.1 = (f32[32,128,128]{2,1,0:T(8,128)S(1)}, f32[32,128,128]{2,1,0:T(8,128)}, u32[]{:S(2)}) copy-start(f32[32,128,128]{2,1,0:T(8,128)} %copy-done) | copy-start | bytes 6291460
  96.3 4.3 %collective-permute-start.1 = (f32[16,128,128]{2,1,0:T(8,128)S(1)}, f32[16,128,128]{2,1,0:T(8,128)S(1)}, u32[]{:S(2)}, u32[]{:S(2)}) collective-permute-start(f32[16,128,128]{2,1,0:T(8,128)S(1)} %get-tuple-element.21), channel_id=1, source_target_pairs={{0,16},{16,0},{32,48},{48,32},{64,80},{80,64},{96,112},{112,96},{1... | collective-permute-start | bytes 3145736 | tf_op jit(solution)/shard_map/ppermute | solution.py:518
  101.2 10.9 %collective-permute-start.2 = (f32[4,128,128]{2,1,0:T(8,128)S(1)}, f32[4,128,128]{2,1,0:T(8,128)S(1)}, u32[]{:S(2)}, u32[]{:S(2)}) collective-permute-start(f32[4,128,128]{2,1,0:T(8,128)S(1)} %get-tuple-element.23), channel_id=1, source_target_pairs={{0,32},{16,48},{32,64},{48,80},{64,96},{80,112},{96,0},{112,16},{1... | collective-permute-start | bytes 786440 | tf_op jit(solution)/shard_map/ppermute | solution.py:514
  101.3 17.6 %collective-permute-start.3 = (f32[4,128,128]{2,1,0:T(8,128)S(1)}, f32[4,128,128]{2,1,0:T(8,128)S(1)}, u32[]{:S(2)}, u32[]{:S(2)}) collective-permute-start(f32[4,128,128]{2,1,0:T(8,128)S(1)} %get-tuple-element.24), channel_id=1, source_target_pairs={{0,64},{16,80},{32,96},{48,112},{64,0},{80,16},{96,32},{112,48},{1... | collective-permute-start | bytes 786440 | tf_op jit(solution)/shard_map/ppermute | solution.py:514
  106.6 12.3 %collective-permute-start.4 = (f32[4,128,128]{2,1,0:T(8,128)S(1)}, f32[4,128,128]{2,1,0:T(8,128)S(1)}, u32[]{:S(2)}, u32[]{:S(2)}) collective-permute-start(f32[4,128,128]{2,1,0:T(8,128)S(1)} %get-tuple-element.25), channel_id=1, source_target_pairs={{0,96},{16,112},{32,0},{48,16},{64,32},{80,48},{96,64},{112,80},{1... | collective-permute-start | bytes 786440 | tf_op jit(solution)/shard_map/ppermute | solution.py:514
  128.8 13.6 %collective-permute-start.7 = (f32[4,128,128]{2,1,0:T(8,128)S(1)}, f32[4,128,128]{2,1,0:T(8,128)S(1)}, u32[]{:S(2)}, u32[]{:S(2)}) collective-permute-start(f32[4,128,128]{2,1,0:T(8,128)S(1)} %factor.1.refs_0_), channel_id=1, source_target_pairs={{0,96},{16,112},{32,0},{48,16},{64,32},{80,48},{96,64},{112,80},{1... | collective-permute-start | bytes 786440 | tf_op jit(solution)/shard_map/ppermute | solution.py:514
  131.1 11.4 %collective-permute-start.6 = (f32[4,128,128]{2,1,0:T(8,128)S(1)}, f32[4,128,128]{2,1,0:T(8,128)S(1)}, u32[]{:S(2)}, u32[]{:S(2)}) collective-permute-start(f32[4,128,128]{2,1,0:T(8,128)S(1)} %factor.1.refs_0_), channel_id=1, source_target_pairs={{0,64},{16,80},{32,96},{48,112},{64,0},{80,16},{96,32},{112,48},{1... | collective-permute-start | bytes 786440 | tf_op jit(solution)/shard_map/ppermute | solution.py:514
  131.1 14.8 %collective-permute-start.5 = (f32[4,128,128]{2,1,0:T(8,128)S(1)}, f32[4,128,128]{2,1,0:T(8,128)S(1)}, u32[]{:S(2)}, u32[]{:S(2)}) collective-permute-start(f32[4,128,128]{2,1,0:T(8,128)S(1)} %factor.1.refs_0_), channel_id=1, source_target_pairs={{0,32},{16,48},{32,64},{48,80},{64,96},{80,112},{96,0},{112,16},{1... | collective-permute-start | bytes 786440 | tf_op jit(solution)/shard_map/ppermute | solution.py:514
  132.0 13.9 %collective-permute-start.8 = (f32[4,128,128]{2,1,0:T(8,128)S(1)}, f32[4,128,128]{2,1,0:T(8,128)S(1)}, u32[]{:S(2)}, u32[]{:S(2)}) collective-permute-start(f32[4,128,128]{2,1,0:T(8,128)S(1)} %factor.1.refs_0_), channel_id=1, source_target_pairs={{0,16},{16,0},{32,48},{48,32},{64,80},{80,64},{96,112},{112,96},{1... | collective-permute-start | bytes 786440 | tf_op jit(solution)/shard_map/ppermute | solution.py:518
  142.5 3.4 %collective-permute-start.11 = (f32[4,128,128]{2,1,0:T(8,128)S(1)}, f32[4,128,128]{2,1,0:T(8,128)S(1)}, u32[]{:S(2)}, u32[]{:S(2)}) collective-permute-start(f32[4,128,128]{2,1,0:T(8,128)S(1)} %collective-permute-done.7.refs_3_), channel_id=1, source_target_pairs={{0,16},{16,0},{32,48},{48,32},{64,80},{80,64},{96,112},{112,96},{1... | collective-permute-start | bytes 786440 | tf_op jit(solution)/shard_map/ppermute | solution.py:518
  142.5 3.4 %collective-permute-start.10 = (f32[4,128,128]{2,1,0:T(8,128)S(1)}, f32[4,128,128]{2,1,0:T(8,128)S(1)}, u32[]{:S(2)}, u32[]{:S(2)}) collective-permute-start(f32[4,128,128]{2,1,0:T(8,128)S(1)} %collective-permute-done.6.refs_2_), channel_id=1, source_target_pairs={{0,16},{16,0},{32,48},{48,32},{64,80},{80,64},{96,112},{112,96},{1... | collective-permute-start | bytes 786440 | tf_op jit(solution)/shard_map/ppermute | solution.py:518
  145.9 1.5 %collective-permute-start.9 = (f32[4,128,128]{2,1,0:T(8,128)S(1)}, f32[4,128,128]{2,1,0:T(8,128)S(1)}, u32[]{:S(2)}, u32[]{:S(2)}) collective-permute-start(f32[4,128,128]{2,1,0:T(8,128)S(1)} %collective-permute-done.5.refs_1_), channel_id=1, source_target_pairs={{0,16},{16,0},{32,48},{48,32},{64,80},{80,64},{96,112},{112,96},{1... | collective-permute-start | bytes 786440 | tf_op jit(solution)/shard_map/ppermute | solution.py:518

commit v4 on v3

--- a/solution.py
+++ b/solution.py
@@ -401,39 +401,26 @@
     return later
 
 
-def factor_kernel(scaling, *refs):
-    out_ref, gre_ref, gim_ref, fre_ref, fim_ref = refs[-5:]
-    ins = refs[:-5]
-    count = out_ref.shape[0]
-    row = lax.broadcasted_iota(jnp.int32, (128, 128), 0)
-    column = lax.broadcasted_iota(jnp.int32, (128, 128), 1)
-    for n in range(count):
-        packed = ins[0][n]
-        for more in ins[1:]:
-            packed = packed + more[n]
-        packed = packed * scaling
-        turned = packed.T
-        gre_ref[n] = jnp.where(row <= column, packed, turned)
-        gim_ref[n] = jnp.where(row < column, -turned, jnp.where(row > column, packed, 0.0))
-    dims = (((0,), (0,)), ((), ()))
-    dot = functools.partial(
-        lax.dot_general,
-        dimension_numbers=dims,
-        preferred_element_type=F32,
-        precision=lax.Precision.HIGHEST,
-    )
-    for offset in range(0, 128, STRIP):
+def factor_strips(offsets, count, gre_ref, gim_ref, fre_ref, fim_ref):
+    base = offsets[0]
+    for offset in offsets:
         strips = []
         for n in range(count):
-            re = gre_ref[n, offset : offset + STRIP]
-            im = gim_ref[n, offset : offset + STRIP]
+            here = slice(offset - base, offset - base + STRIP)
+            re, im = gre_ref[n, here], gim_ref[n, here]
             if offset:
                 fr, fi = fre_ref[n, :offset], fim_ref[n, :offset]
                 lr, li = fr[:, offset : offset + STRIP], fi[:, offset : offset + STRIP]
                 left = jnp.concatenate(
                     [jnp.concatenate([lr, -li], 1), jnp.concatenate([li, lr], 1)], 0
                 )
-                update = dot(left, jnp.concatenate([fr, fi], 0))
+                update = lax.dot_general(
+                    left,
+                    jnp.concatenate([fr, fi], 0),
+                    dimension_numbers=(((0,), (0,)), ((), ())),
+                    preferred_element_type=F32,
+                    precision=lax.Precision.HIGHEST,
+                )
                 re = re - update[:STRIP]
                 im = im - update[STRIP:]
             strips.append([(re[8 * g : 8 * g + 8], im[8 * g : 8 * g + 8]) for g in range(STRIP // 8)])
@@ -451,28 +438,107 @@
             here = slice(offset, offset + STRIP)
             fre_ref[n, here] = jnp.where(c >= r, fre_ref[n, here], 0.0)
             fim_ref[n, here] = jnp.where(c > r, fim_ref[n, here], 0.0)
+
+
+def iota64():
+    shape = (64, 128)
+    return lax.broadcasted_iota(jnp.int32, shape, 0), lax.broadcasted_iota(jnp.int32, shape, 1)
+
+
+def flip_blocks(value):
+    turned = value.T
+    return jnp.concatenate([turned[:64], turned[64:]], 1)
+
+
+def top_kernel(scaling, *refs):
+    ins = refs[:4]
+    right_ref, side_ref, gre_ref, gim_ref, fre_ref, fim_ref = refs[4:]
+    count = right_ref.shape[0]
+    r, c = iota64()
     for n in range(count):
-        out_ref[n] = fre_ref[n] + fim_ref[n].T
-
-
-def factor(pieces, scaling):
+        packed = ins[0][n]
+        for more in ins[1:]:
+            packed = packed + more[n]
+        packed = packed * scaling
+        upper = packed[:64]
+        turned = packed[:, :64].T
+        gre_ref[n] = jnp.where(r <= c, upper, turned)
+        gim_ref[n] = jnp.where(r < c, -turned, jnp.where(r > c, upper, 0.0))
+        side_ref[n] = packed[64:]
+    factor_strips((0, STRIP), count, gre_ref, gim_ref, fre_ref, fim_ref)
+    for n in range(count):
+        re, im = fre_ref[n], fim_ref[n]
+        right_ref[n] = jnp.where(c < 64, pltpu.roll(im, 64, 1), re)
+        corner = jnp.where(r <= c, re, flip_blocks(im))
+        side_ref[n] = jnp.where(c < 64, corner, side_ref[n])
+
+
+def bottom_kernel(right_ref, side_ref, out_ref, gre_ref, gim_ref, fre_ref, fim_ref):
+    count = right_ref.shape[0]
+    r, c = iota64()
+    for n in range(count):
+        right, side = right_ref[n], side_ref[n]
+        fre_ref[n, :64] = jnp.where(c < 64, 0.0, right)
+        fim_ref[n, :64] = jnp.where(c < 64, 0.0, pltpu.roll(right, 64, 1))
+        turned = flip_blocks(side)
+        gre_ref[n] = jnp.where(r <= c - 64, side, turned)
+        gim_ref[n] = jnp.where(r < c - 64, -turned, jnp.where(r > c - 64, side, 0.0))
+    factor_strips((64, 64 + STRIP), count, gre_ref, gim_ref, fre_ref, fim_ref)
+    for n in range(count):
+        re, im = fre_ref[n, 64:], fim_ref[n, 64:]
+        corner = jnp.where(r <= c - 64, re, flip_blocks(im))
+        out_ref[n] = jnp.where(c < 64, side_ref[n], corner)
+
+
+def factor_top(pieces, scaling):
     count = pieces[0].shape[0]
-    return pl.pallas_call(
-        functools.partial(factor_kernel, scaling),
-        in_specs=[VMEM] * len(pieces),
-        out_specs=VMEM,
-        out_shape=jax.ShapeDtypeStruct((count, 128, 128), F32),
-        scratch_shapes=[pltpu.VMEM((count, 128, 128), F32)] * 4,
+    piece = jax.ShapeDtypeStruct((count, 64, 128), F32)
+    return pl.pallas_call(
+        functools.partial(top_kernel, scaling),
+        in_specs=[VMEM] * 4,
+        out_specs=[VMEM] * 2,
+        out_shape=[piece] * 2,
+        scratch_shapes=[pltpu.VMEM((count, 64, 128), F32)] * 4,
         compiler_params=params(16),
         cost_estimate=cost(1e6, 1e5),
-        name="factor",
+        name="factor_top",
     )(*pieces)
 
 
+def factor_bottom(right, side):
+    count = right.shape[0]
+    return pl.pallas_call(
+        bottom_kernel,
+        in_specs=[VMEM] * 2,
+        out_specs=VMEM,
+        out_shape=jax.ShapeDtypeStruct((count, 64, 128), F32),
+        scratch_shapes=[pltpu.VMEM((count, 64, 128), F32)] * 2 + [pltpu.VMEM((count, 128, 128), F32)] * 2,
+        compiler_params=params(16),
+        cost_estimate=cost(1e6, 1e5),
+        name="factor_bottom",
+    )(right, side)
+
+
+def hold_kernel(*refs):
+    pass
+
+
+def hold(value, until):
+    return pl.pallas_call(
+        hold_kernel,
+        in_specs=[ANY] * (1 + len(until)),
+        out_specs=ANY,
+        out_shape=jax.ShapeDtypeStruct(value.shape, value.dtype),
+        input_output_aliases={0: 0},
+        compiler_params=params(16),
+        cost_estimate=cost(1e3, 1e3),
+        name="hold",
+    )(value, *until)
+
+
 def unpack_kernel(share, spot_ref, *refs):
-    pieces, out_ref, held_ref, sems = refs[:8], refs[8], refs[9], refs[10]
-    row = lax.broadcasted_iota(jnp.int32, (128, 128), 0)
-    column = lax.broadcasted_iota(jnp.int32, (128, 128), 1)
+    rights, corners, out_ref, held_ref, sems = refs[:8], refs[8:16], refs[16], refs[17], refs[18]
+    r, c = iota64()
     y, core = spot_ref[0], spot_ref[1]
     copies = []
     for k in range(8):
@@ -481,9 +547,15 @@
         whose = core + other - 2 * core * other
         base = (whose * 4 + owner) * share
         for i in range(share):
-            packed = pieces[k][i]
-            held_ref[k * share + i, 0] = jnp.where(row <= column, packed, 0.0)
-            held_ref[k * share + i, 1] = jnp.where(row < column, packed.T, 0.0)
+            right, corner = rights[k][i], corners[k][i]
+            turned = flip_blocks(corner)
+            place = k * share + i
+            held_ref[place, 0, 0:64] = jnp.where(c < 64, jnp.where(r <= c, corner, 0.0), right)
+            held_ref[place, 1, 0:64] = jnp.where(
+                c < 64, jnp.where(r < c, turned, 0.0), pltpu.roll(right, 64, 1)
+            )
+            held_ref[place, 0, 64:128] = jnp.where(r <= c - 64, corner, 0.0)
+            held_ref[place, 1, 64:128] = jnp.where(r < c - 64, turned, 0.0)
         copy = pltpu.make_async_copy(
             held_ref.at[pl.ds(k * share, share)], out_ref.at[pl.ds(base, share)], sems.at[k]
         )
@@ -493,11 +565,11 @@
         copy.wait()
 
 
-def unpack(spot, pieces):
-    share = pieces[0].shape[0]
+def unpack(spot, rights, corners):
+    share = rights[0].shape[0]
     return pl.pallas_call(
         functools.partial(unpack_kernel, share),
-        in_specs=[SMEM] + [VMEM] * 8,
+        in_specs=[SMEM] + [VMEM] * 16,
         out_specs=ANY,
         out_shape=jax.ShapeDtypeStruct((BINS, 2, 128, 128), F32),
         scratch_shapes=[
@@ -507,7 +579,7 @@
         compiler_params=params(16),
         cost_estimate=cost(1e6, 1e5),
         name="unpack",
-    )(spot, *pieces)
+    )(spot, *rights, *corners)
 
 
 def along_y(value, steps):
@@ -546,8 +618,10 @@
     sums0, spectra = gram0(mask, got0)
     send, spectra = gram1(True, spot, mask, got1, sums0, spectra, "gram1_send")
     keep, spectra = gram1(False, spot, mask, got1, sums0, spectra, "gram1_keep")
-    mine = factor(gather_sums(spot, keep, send), scaling)
-    factors = unpack(spot, share_factors(mine))
+    right, side = factor_top(gather_sums(spot, keep, send), scaling)
+    rights = share_factors(right)
+    corners = share_factors(hold(factor_bottom(right, side), rights[1:4]))
+    factors = unpack(spot, rights, corners)
     return spectra, factors
 
 

time: 152 us -> 152 us (level)
  waiting for transfers between devices: 73.3 us -> 68.8 us
  starting transfers between devices: 25.5 us -> 28.9 us
    ppermute x6 -> x9, waiting for transfers between devices: 25.6 us -> 21.3 us  [along_y(): lax.ppermute(value, 'range', [(i, (i + 2 * steps) % 8) for i in range(8)])]
    ppermute x6 -> x9, starting transfers between devices: 8.54 us -> 11.1 us  [along_y(): lax.ppermute(value, 'range', [(i, (i + 2 * steps) % 8) for i in range(8)])]
    pallas_call x1 -> x3, Pallas kernels: 9.95 us -> 10.3 us  [the longest x1 5.55 us: factor_bottom(): pl.pallas_call(bottom_kernel, in_specs=[VMEM] * 2, out_specs=VMEM, out_sh...]
  transfers between devices with their start and end apart: 14 -> 21, of which waited for: 7 -> 10; matrix products, arithmetic and copies ran while one was open for 0% -> 0% of each run, Pallas kernels for 12% -> 16%
where the time goes in v4:
time: 152 us; the launch traced here: 150 us
  waiting for transfers between devices  68.8 us (45%)
  Pallas kernels  45.6 us (30%)
  starting transfers between devices  28.9 us (19%)
  local copies, waits for them, and re-layouts  5.86 us (4%)
    all_to_all x2, waiting for transfers between devices, across(): lax.all_to_all(value, 'chan', split_axis=0, concat_axis=0, tiled=True)  46.2 us
    ppermute x9, waiting for transfers between devices, along_y(): lax.ppermute(value, 'range', [(i, (i + 2 * steps) % 8) for i in range(8)])  21.3 us
    all_to_all x2, starting transfers between devices, across(): lax.all_to_all(value, 'chan', split_axis=0, concat_axis=0, tiled=True)  15.2 us
    ppermute x9, starting transfers between devices, along_y(): lax.ppermute(value, 'range', [(i, (i + 2 * steps) % 8) for i in range(8)])  11.1 us
    pallas_call x1, Pallas kernels, front0(): pl.pallas_call(front0_kernel, grid=(2,), in_specs=[pl.BlockSpec(chirp.sha...  8.51 us
    pallas_call x2, Pallas kernels, gram1(): pl.pallas_call(functools.partial(gram1_kernel, other), grid_spec=pltpu.Pr...  8.51 us
    pallas_call x1, Pallas kernels, front1(): pl.pallas_call(front1_kernel, grid=(2,), in_specs=[pl.BlockSpec(chirp.sha...  8.13 us
    pallas_call x1, Pallas kernels, gram0(): pl.pallas_call(gram0_kernel, grid=(BINS // GROUP,), in_specs=[SMEM, pl.Bl...  6.16 us
  transfers between devices with their start and end apart: 21, of which 10 were waited for; matrix products, arithmetic and copies ran while one was open for 0% of the time, Pallas kernels for 16%

profile of v4, /device:TPU:0, one launch (start us, length us, event | category | flops | bytes accessed | tf_op | source)
XLA Modules:
  0.0 150.2 jit_solution(7846633974607294575)
XLA Ops:
  0.6 8.5 %front0.1 = (f32[4224,128]{1,0:T(8,128)}, f32[2,4,512,128]{3,2,1,0:T(8,128)}) custom-call(f32[2,129]{1,0:T(2,128)} %chirp_ref.3, f32[2,4,512,256]{3,2,1,0:T(8,128)} %x_ref.3, bf16[2,4,256,256]{3,2,1,0:T(8,128)(2,1)} %constant.10.clone.w_ref), custom_call_target="tpu_custom_call" | custom-call | flops 4000000000 | bytes 12000000 | tf_op jit(solution)/shard_map/front0/pallas_call | solution.py:155
  10.4 8.0 %all-to-all-start.1 = ((f32[16,33,8,128]{3,2,1,0:T(8,128)}), f32[16,33,8,128]{3,2,1,0:T(8,128)S(1)}, u32[]{:S(2)}, u32[]{:S(2)}) async-start(f32[16,33,8,128]{3,2,1,0:T(8,128)} %bitcast.9), calls=%async_computation.1 | async-start | bytes 4325376 | tf_op jit(solution)/shard_map/all_to_all | solution.py:594
  18.4 8.1 %front1.1 = f32[4224,128]{1,0:T(8,128)} custom-call(f32[2,129]{1,0:T(2,128)} %chirp_ref.3, f32[2,4,512,256]{3,2,1,0:T(8,128)} %x_ref.3, f32[2,4,512,128]{3,2,1,0:T(8,128)} %collective-permute-done.h_ref, bf16[2,4,256,256]{3,2,1,0:T(8,128)(2,1)} %constant.10.clone.w_ref), custom_call_target="tpu_custom_call" | custom-call | flops 4000000000 | bytes 8000000 | tf_op jit(solution)/shard_map/front1/pallas_call | solution.py:179
  26.5 23.8 %all-to-all-done.1.r_ref.edge_ref = f32[16,33,8,128]{3,2,1,0:T(8,128)S(1)} async-done(((f32[16,33,8,128]{3,2,1,0:T(8,128)}), f32[16,33,8,128]{3,2,1,0:T(8,128)S(1)}, u32[]{:S(2)}, u32[]{:S(2)}) %all-to-all-start.1) | async-done | bytes 2162720 | tf_op jit(solution)/shard_map/all_to_all | solution.py:594
  50.4 1.3 copy-done.2
  51.7 7.2 %all-to-all-start = ((f32[16,33,8,128]{3,2,1,0:T(8,128)}), f32[16,33,8,128]{3,2,1,0:T(8,128)S(1)}, u32[]{:S(2)}, u32[]{:S(2)}) async-start(f32[16,33,8,128]{3,2,1,0:T(8,128)} %bitcast.8), calls=%async_computation | async-start | bytes 4325376 | tf_op jit(solution)/shard_map/all_to_all | solution.py:594
  59.0 1.6 %copy-done.3 = f32[16,33,8,128]{3,2,1,0:T(8,128)S(1)} copy-done((f32[16,33,8,128]{3,2,1,0:T(8,128)S(1)}, f32[16,33,8,128]{3,2,1,0:T(8,128)}, u32[]{:S(2)}) %copy-start.3) | copy-done | bytes 2162712
  60.6 6.2 %gram0.1 = (f32[32,128,128]{2,1,0:T(8,128)S(1)}, bf16[2,32,64,256]{3,2,1,0:T(8,128)(2,1)}) custom-call(s32[2,32]{1,0:T(2,128)S(1)} %bitcast.5, f32[16,33,8,128]{3,2,1,0:T(8,128)S(1)} %copy-done.3, f32[16,33,8,128]{3,2,1,0:T(8,128)S(1)} %copy-done.3), custom_call_target="tpu_custom_call" | custom-call | flops 2000000000 | bytes 6000000 | tf_op jit(solution)/shard_map/gram0/pallas_call | solution.py:256
  66.8 1.3 copy-done
  68.1 22.3 %all-to-all-done.r_ref.edge_ref = f32[16,33,8,128]{3,2,1,0:T(8,128)S(1)} async-done(((f32[16,33,8,128]{3,2,1,0:T(8,128)}), f32[16,33,8,128]{3,2,1,0:T(8,128)S(1)}, u32[]{:S(2)}, u32[]{:S(2)}) %all-to-all-start) | async-done | bytes 2162720 | tf_op jit(solution)/shard_map/all_to_all | solution.py:594
  90.4 1.6 %copy-done.1 = f32[32,128,128]{2,1,0:T(8,128)S(1)} copy-done((f32[32,128,128]{2,1,0:T(8,128)S(1)}, f32[32,128,128]{2,1,0:T(8,128)}, u32[]{:S(2)}) %copy-start.1) | copy-done | bytes 2097176
  92.0 4.2 %gram1_send.1 = (f32[16,128,128]{2,1,0:T(8,128)S(1)}, bf16[2,32,64,256]{3,2,1,0:T(8,128)(2,1)}) custom-call(s32[2]{0:T(128)S(1)} %pad_add_fusion.spot_ref, s32[2,32]{1,0:T(2,128)S(1)} %bitcast.6, f32[16,33,8,128]{3,2,1,0:T(8,128)S(1)} %all-to-all-done.r_ref.edge_ref, ...), custom_call_target="tpu_custom_call", output_to_operand_aliasing={{1}: (5, {})} | custom-call | flops 2000000000 | bytes 6000000 | tf_op jit(solution)/shard_map/gram1_send/pallas_call | solution.py:295
  96.3 4.3 %gram1_keep.1 = (f32[16,128,128]{2,1,0:T(8,128)S(1)}, bf16[2,32,64,256]{3,2,1,0:T(8,128)(2,1)}) custom-call(s32[2]{0:T(128)S(1)} %pad_add_fusion.spot_ref, s32[2,32]{1,0:T(2,128)S(1)} %bitcast.7, f32[16,33,8,128]{3,2,1,0:T(8,128)S(1)} %all-to-all-done.r_ref.edge_ref, ...), custom_call_target="tpu_custom_call", output_to_operand_aliasing={{1}: (5, {})} | custom-call | flops 2000000000 | bytes 6000000 | tf_op jit(solution)/shard_map/gram1_keep/pallas_call | solution.py:295
  101.3 5.2 %collective-permute-start.3 = (f32[4,128,128]{2,1,0:T(8,128)S(1)}, f32[4,128,128]{2,1,0:T(8,128)S(1)}, u32[]{:S(2)}, u32[]{:S(2)}) collective-permute-start(f32[4,128,128]{2,1,0:T(8,128)S(1)} %get-tuple-element.26), channel_id=1, source_target_pairs={{0,64},{16,80},{32,96},{48,112},{64,0},{80,16},{96,32},{112,48},{1... | collective-permute-start | bytes 786440 | tf_op jit(solution)/shard_map/ppermute | solution.py:586
  106.5 5.5 %collective-permute-done.2.refs_1_ = f32[4,128,128]{2,1,0:T(8,128)S(1)} collective-permute-done((f32[4,128,128]{2,1,0:T(8,128)S(1)}, f32[4,128,128]{2,1,0:T(8,128)S(1)}, u32[]{:S(2)}, u32[]{:S(2)}) %collective-permute-start.2) | collective-permute-done | bytes 262176 | tf_op jit(solution)/shard_map/ppermute | solution.py:586
  112.0 6.8 %collective-permute-done.3.refs_2_ = f32[4,128,128]{2,1,0:T(8,128)S(1)} collective-permute-done((f32[4,128,128]{2,1,0:T(8,128)S(1)}, f32[4,128,128]{2,1,0:T(8,128)S(1)}, u32[]{:S(2)}, u32[]{:S(2)}) %collective-permute-start.3) | collective-permute-done | bytes 262176 | tf_op jit(solution)/shard_map/ppermute | solution.py:586
  118.8 4.8 %factor_top.1 = (f32[4,64,128]{2,1,0:T(8,128)S(1)}, f32[4,64,128]{2,1,0:T(8,128)S(1)}) custom-call(f32[4,128,128]{2,1,0:T(8,128)S(1)} %get-tuple-element.24.refs_0_, f32[4,128,128]{2,1,0:T(8,128)S(1)} %collective-permute-done.2.refs_1_, f32[4,128,128]{2,1,0:T(8,128)S(1)} %collective-permute-done.3.refs_2_, f32[4,128,128]{2,1,0:T(8,128)S(1)} %collective-permute-done.4.refs_3_), custom_call_target="tpu_custom_call" | custom-call | flops 1000000 | bytes 100000 | tf_op jit(solution)/shard_map/factor_top/pallas_call | solution.py:496
  123.6 2.2 %collective-permute-start.7 = (f32[4,64,128]{2,1,0:T(8,128)S(1)}, f32[4,64,128]{2,1,0:T(8,128)S(1)}, u32[]{:S(2)}, u32[]{:S(2)}) collective-permute-start(f32[4,64,128]{2,1,0:T(8,128)S(1)} %get-tuple-element.28.right_ref.refs_0_), channel_id=1, source_target_pairs={{0,96},{16,112},{32,0},{48,16},{64,32},{80,48},{96,64},{112,80},{1... | collective-permute-start | bytes 393224 | tf_op jit(solution)/shard_map/ppermute | solution.py:586
  126.7 5.5 %factor_bottom.1.refs_0_ = f32[4,64,128]{2,1,0:T(8,128)S(1)} custom-call(f32[4,64,128]{2,1,0:T(8,128)S(1)} %get-tuple-element.28.right_ref.refs_0_, f32[4,64,128]{2,1,0:T(8,128)S(1)} %get-tuple-element.29.side_ref), custom_call_target="tpu_custom_call" | custom-call | flops 1000000 | bytes 100000 | tf_op jit(solution)/shard_map/factor_bottom/pallas_call | solution.py:510
  135.9 1.7 %collective-permute-start.13 = (f32[4,64,128]{2,1,0:T(8,128)S(1)}, f32[4,64,128]{2,1,0:T(8,128)S(1)}, u32[]{:S(2)}, u32[]{:S(2)}) collective-permute-start(f32[4,64,128]{2,1,0:T(8,128)S(1)} %hold.1.refs_8_), channel_id=1, source_target_pairs={{0,64},{16,80},{32,96},{48,112},{64,0},{80,16},{96,32},{112,48},{1... | collective-permute-start | bytes 393224 | tf_op jit(solution)/shard_map/ppermute | solution.py:586
  138.4 2.9 %collective-permute-done.14.refs_11_ = f32[4,64,128]{2,1,0:T(8,128)S(1)} collective-permute-done((f32[4,64,128]{2,1,0:T(8,128)S(1)}, f32[4,64,128]{2,1,0:T(8,128)S(1)}, u32[]{:S(2)}, u32[]{:S(2)}) %collective-permute-start.14) | collective-permute-done | bytes 131104 | tf_op jit(solution)/shard_map/ppermute | solution.py:586
  141.4 2.4 %collective-permute-done.13.refs_10_ = f32[4,64,128]{2,1,0:T(8,128)S(1)} collective-permute-done((f32[4,64,128]{2,1,0:T(8,128)S(1)}, f32[4,64,128]{2,1,0:T(8,128)S(1)}, u32[]{:S(2)}, u32[]{:S(2)}) %collective-permute-start.13) | collective-permute-done | bytes 131104 | tf_op jit(solution)/shard_map/ppermute | solution.py:586
  143.8 1.6 %collective-permute-done.12.refs_9_ = f32[4,64,128]{2,1,0:T(8,128)S(1)} collective-permute-done((f32[4,64,128]{2,1,0:T(8,128)S(1)}, f32[4,64,128]{2,1,0:T(8,128)S(1)}, u32[]{:S(2)}, u32[]{:S(2)}) %collective-permute-start.12) | collective-permute-done | bytes 131104 | tf_op jit(solution)/shard_map/ppermute | solution.py:586
  146.7 3.3 %unpack.1 = f32[32,2,128,128]{3,2,1,0:T(8,128)} custom-call(s32[2]{0:T(128)S(1)} %pad_add_fusion.spot_ref, f32[4,64,128]{2,1,0:T(8,128)S(1)} %get-tuple-element.28.right_ref.refs_0_, f32[4,64,128]{2,1,0:T(8,128)S(1)} %collective-permute-done.5.refs_1_, f32[4,64,128]{2,1,0:T(8,128)S(1)} %collective-permute-done.6.refs_2_, ...), custom_call_target="tpu_custom_call" | custom-call | flops 1000000 | bytes 100000 | tf_op jit(solution)/shard_map/unpack/pallas_call | solution.py:570
  (39 shorter events, 8.8 us)
Async XLA Ops:
  9.1 9.3 %collective-permute-start = (f32[2,4,512,128]{3,2,1,0:T(8,128)}, f32[2,4,512,128]{3,2,1,0:T(8,128)}, u32[]{:S(2)}, u32[]{:S(2)}) collective-permute-start(f32[2,4,512,128]{3,2,1,0:T(8,128)} %get-tuple-element.16), channel_id=1, source_target_pairs={{16,0},{32,16},{48,32},{64,48},{80,64},{96,80},{112,96},{17,1},{33... | collective-permute-start | bytes 6291464 | tf_op jit(solution)/shard_map/ppermute | solution.py:615
  10.4 40.0 %all-to-all-start.1 = ((f32[16,33,8,128]{3,2,1,0:T(8,128)}), f32[16,33,8,128]{3,2,1,0:T(8,128)S(1)}, u32[]{:S(2)}, u32[]{:S(2)}) async-start(f32[16,33,8,128]{3,2,1,0:T(8,128)} %bitcast.9), calls=%async_computation.1 | async-start | bytes 4325376 | tf_op jit(solution)/shard_map/all_to_all | solution.py:594
  51.7 7.3 %copy-start.4 = (s32[32,2]{0,1:T(2,128)S(1)}, s32[32,2]{0,1:T(2,128)}, u32[]{:S(2)}) copy-start(s32[32,2]{0,1:T(2,128)} %param.6) | copy-start | bytes 772
  51.7 38.7 %all-to-all-start = ((f32[16,33,8,128]{3,2,1,0:T(8,128)}), f32[16,33,8,128]{3,2,1,0:T(8,128)S(1)}, u32[]{:S(2)}, u32[]{:S(2)}) async-start(f32[16,33,8,128]{3,2,1,0:T(8,128)} %bitcast.8), calls=%async_computation | async-start | bytes 4325376 | tf_op jit(solution)/shard_map/all_to_all | solution.py:594
  59.0 1.6 %copy-start.3 = (f32[16,33,8,128]{3,2,1,0:T(8,128)S(1)}, f32[16,33,8,128]{3,2,1,0:T(8,128)}, u32[]{:S(2)}) copy-start(f32[16,33,8,128]{3,2,1,0:T(8,128)} %copy-done.2) | copy-start | bytes 6488068
  90.4 1.6 %copy-start.1 = (f32[32,128,128]{2,1,0:T(8,128)S(1)}, f32[32,128,128]{2,1,0:T(8,128)}, u32[]{:S(2)}) copy-start(f32[32,128,128]{2,1,0:T(8,128)} %copy-done) | copy-start | bytes 6291460
  96.3 4.3 %collective-permute-start.1 = (f32[16,128,128]{2,1,0:T(8,128)S(1)}, f32[16,128,128]{2,1,0:T(8,128)S(1)}, u32[]{:S(2)}, u32[]{:S(2)}) collective-permute-start(f32[16,128,128]{2,1,0:T(8,128)S(1)} %get-tuple-element.23), channel_id=1, source_target_pairs={{0,16},{16,0},{32,48},{48,32},{64,80},{80,64},{96,112},{112,96},{1... | collective-permute-start | bytes 3145736 | tf_op jit(solution)/shard_map/ppermute | solution.py:590
  101.2 10.8 %collective-permute-start.2 = (f32[4,128,128]{2,1,0:T(8,128)S(1)}, f32[4,128,128]{2,1,0:T(8,128)S(1)}, u32[]{:S(2)}, u32[]{:S(2)}) collective-permute-start(f32[4,128,128]{2,1,0:T(8,128)S(1)} %get-tuple-element.25), channel_id=1, source_target_pairs={{0,32},{16,48},{32,64},{48,80},{64,96},{80,112},{96,0},{112,16},{1... | collective-permute-start | bytes 786440 | tf_op jit(solution)/shard_map/ppermute | solution.py:586
  101.3 17.5 %collective-permute-start.3 = (f32[4,128,128]{2,1,0:T(8,128)S(1)}, f32[4,128,128]{2,1,0:T(8,128)S(1)}, u32[]{:S(2)}, u32[]{:S(2)}) collective-permute-start(f32[4,128,128]{2,1,0:T(8,128)S(1)} %get-tuple-element.26), channel_id=1, source_target_pairs={{0,64},{16,80},{32,96},{48,112},{64,0},{80,16},{96,32},{112,48},{1... | collective-permute-start | bytes 786440 | tf_op jit(solution)/shard_map/ppermute | solution.py:586
  106.5 12.3 %collective-permute-start.4 = (f32[4,128,128]{2,1,0:T(8,128)S(1)}, f32[4,128,128]{2,1,0:T(8,128)S(1)}, u32[]{:S(2)}, u32[]{:S(2)}) collective-permute-start(f32[4,128,128]{2,1,0:T(8,128)S(1)} %get-tuple-element.27), channel_id=1, source_target_pairs={{0,96},{16,112},{32,0},{48,16},{64,32},{80,48},{96,64},{112,80},{1... | collective-permute-start | bytes 786440 | tf_op jit(solution)/shard_map/ppermute | solution.py:586
  123.6 8.7 %collective-permute-start.7 = (f32[4,64,128]{2,1,0:T(8,128)S(1)}, f32[4,64,128]{2,1,0:T(8,128)S(1)}, u32[]{:S(2)}, u32[]{:S(2)}) collective-permute-start(f32[4,64,128]{2,1,0:T(8,128)S(1)} %get-tuple-element.28.right_ref.refs_0_), channel_id=1, source_target_pairs={{0,96},{16,112},{32,0},{48,16},{64,32},{80,48},{96,64},{112,80},{1... | collective-permute-start | bytes 393224 | tf_op jit(solution)/shard_map/ppermute | solution.py:586
  125.8 7.9 %collective-permute-start.6 = (f32[4,64,128]{2,1,0:T(8,128)S(1)}, f32[4,64,128]{2,1,0:T(8,128)S(1)}, u32[]{:S(2)}, u32[]{:S(2)}) collective-permute-start(f32[4,64,128]{2,1,0:T(8,128)S(1)} %get-tuple-element.28.right_ref.refs_0_), channel_id=1, source_target_pairs={{0,64},{16,80},{32,96},{48,112},{64,0},{80,16},{96,32},{112,48},{1... | collective-permute-start | bytes 393224 | tf_op jit(solution)/shard_map/ppermute | solution.py:586
  125.8 9.2 %collective-permute-start.5 = (f32[4,64,128]{2,1,0:T(8,128)S(1)}, f32[4,64,128]{2,1,0:T(8,128)S(1)}, u32[]{:S(2)}, u32[]{:S(2)}) collective-permute-start(f32[4,64,128]{2,1,0:T(8,128)S(1)} %get-tuple-element.28.right_ref.refs_0_), channel_id=1, source_target_pairs={{0,32},{16,48},{32,64},{48,80},{64,96},{80,112},{96,0},{112,16},{1... | collective-permute-start | bytes 393224 | tf_op jit(solution)/shard_map/ppermute | solution.py:586
  126.7 10.9 %collective-permute-start.8 = (f32[4,64,128]{2,1,0:T(8,128)S(1)}, f32[4,64,128]{2,1,0:T(8,128)S(1)}, u32[]{:S(2)}, u32[]{:S(2)}) collective-permute-start(f32[4,64,128]{2,1,0:T(8,128)S(1)} %get-tuple-element.28.right_ref.refs_0_), channel_id=1, source_target_pairs={{0,16},{16,0},{32,48},{48,32},{64,80},{80,64},{96,112},{112,96},{1... | collective-permute-start | bytes 393224 | tf_op jit(solution)/shard_map/ppermute | solution.py:590
  132.3 5.3 %collective-permute-start.11 = (f32[4,64,128]{2,1,0:T(8,128)S(1)}, f32[4,64,128]{2,1,0:T(8,128)S(1)}, u32[]{:S(2)}, u32[]{:S(2)}) collective-permute-start(f32[4,64,128]{2,1,0:T(8,128)S(1)} %collective-permute-done.7.refs_3_), channel_id=1, source_target_pairs={{0,16},{16,0},{32,48},{48,32},{64,80},{80,64},{96,112},{112,96},{1... | collective-permute-start | bytes 393224 | tf_op jit(solution)/shard_map/ppermute | solution.py:590
  133.7 4.3 %collective-permute-start.10 = (f32[4,64,128]{2,1,0:T(8,128)S(1)}, f32[4,64,128]{2,1,0:T(8,128)S(1)}, u32[]{:S(2)}, u32[]{:S(2)}) collective-permute-start(f32[4,64,128]{2,1,0:T(8,128)S(1)} %collective-permute-done.6.refs_2_), channel_id=1, source_target_pairs={{0,16},{16,0},{32,48},{48,32},{64,80},{80,64},{96,112},{112,96},{1... | collective-permute-start | bytes 393224 | tf_op jit(solution)/shard_map/ppermute | solution.py:590
  135.0 6.4 %collective-permute-start.14 = (f32[4,64,128]{2,1,0:T(8,128)S(1)}, f32[4,64,128]{2,1,0:T(8,128)S(1)}, u32[]{:S(2)}, u32[]{:S(2)}) collective-permute-start(f32[4,64,128]{2,1,0:T(8,128)S(1)} %hold.1.refs_8_), channel_id=1, source_target_pairs={{0,96},{16,112},{32,0},{48,16},{64,32},{80,48},{96,64},{112,80},{1... | collective-permute-start | bytes 393224 | tf_op jit(solution)/shard_map/ppermute | solution.py:586
  135.9 7.9 %collective-permute-start.13 = (f32[4,64,128]{2,1,0:T(8,128)S(1)}, f32[4,64,128]{2,1,0:T(8,128)S(1)}, u32[]{:S(2)}, u32[]{:S(2)}) collective-permute-start(f32[4,64,128]{2,1,0:T(8,128)S(1)} %hold.1.refs_8_), channel_id=1, source_target_pairs={{0,64},{16,80},{32,96},{48,112},{64,0},{80,16},{96,32},{112,48},{1... | collective-permute-start | bytes 393224 | tf_op jit(solution)/shard_map/ppermute | solution.py:586
  137.6 7.7 %collective-permute-start.12 = (f32[4,64,128]{2,1,0:T(8,128)S(1)}, f32[4,64,128]{2,1,0:T(8,128)S(1)}, u32[]{:S(2)}, u32[]{:S(2)}) collective-permute-start(f32[4,64,128]{2,1,0:T(8,128)S(1)} %hold.1.refs_8_), channel_id=1, source_target_pairs={{0,32},{16,48},{32,64},{48,80},{64,96},{80,112},{96,0},{112,16},{1... | collective-permute-start | bytes 393224 | tf_op jit(solution)/shard_map/ppermute | solution.py:586
  137.6 7.7 %collective-permute-start.15 = (f32[4,64,128]{2,1,0:T(8,128)S(1)}, f32[4,64,128]{2,1,0:T(8,128)S(1)}, u32[]{:S(2)}, u32[]{:S(2)}) collective-permute-start(f32[4,64,128]{2,1,0:T(8,128)S(1)} %hold.1.refs_8_), channel_id=1, source_target_pairs={{0,16},{16,0},{32,48},{48,32},{64,80},{80,64},{96,112},{112,96},{1... | collective-permute-start | bytes 393224 | tf_op jit(solution)/shard_map/ppermute | solution.py:590
  138.0 7.4 %collective-permute-start.9 = (f32[4,64,128]{2,1,0:T(8,128)S(1)}, f32[4,64,128]{2,1,0:T(8,128)S(1)}, u32[]{:S(2)}, u32[]{:S(2)}) collective-permute-start(f32[4,64,128]{2,1,0:T(8,128)S(1)} %collective-permute-done.5.refs_1_), channel_id=1, source_target_pairs={{0,16},{16,0},{32,48},{48,32},{64,80},{80,64},{96,112},{112,96},{1... | collective-permute-start | bytes 393224 | tf_op jit(solution)/shard_map/ppermute | solution.py:590
  141.4 4.0 %collective-permute-start.18 = (f32[4,64,128]{2,1,0:T(8,128)S(1)}, f32[4,64,128]{2,1,0:T(8,128)S(1)}, u32[]{:S(2)}, u32[]{:S(2)}) collective-permute-start(f32[4,64,128]{2,1,0:T(8,128)S(1)} %collective-permute-done.14.refs_11_), channel_id=1, source_target_pairs={{0,16},{16,0},{32,48},{48,32},{64,80},{80,64},{96,112},{112,96},{1... | collective-permute-start | bytes 393224 | tf_op jit(solution)/shard_map/ppermute | solution.py:590
  143.8 1.6 %collective-permute-start.17 = (f32[4,64,128]{2,1,0:T(8,128)S(1)}, f32[4,64,128]{2,1,0:T(8,128)S(1)}, u32[]{:S(2)}, u32[]{:S(2)}) collective-permute-start(f32[4,64,128]{2,1,0:T(8,128)S(1)} %collective-permute-done.13.refs_10_), channel_id=1, source_target_pairs={{0,16},{16,0},{32,48},{48,32},{64,80},{80,64},{96,112},{112,96},{1... | collective-permute-start | bytes 393224 | tf_op jit(solution)/shard_map/ppermute | solution.py:590
  145.4 1.3 collective-permute-start.16
  (2 other events, 2.7 us)
